TPU v7x, 32 devices: a whole 2x2x4 slice. The times are simulated.
32 devices in a mesh: grp: 2 (over x), row: 8 (over z, y), col: 2 (over core).
Axes of the slice: x: 2, y: 2, z: 4, core: 2. Of those that a mesh axis runs over, the one named last changes fastest.
Arguments:
- geometry: bfloat16 [32, 7, 1024], P(('grp', 'row'), None, 'col'), parts along dimension 0, may hold values from -0.5 to 4, as said below
- currents: bfloat16 [32, 64, 1024], P(('grp', 'row'), None, 'col'), parts along dimension 0, may hold values from -6 to 6
- pair_count: int32 [32], P('grp'), parts along dimension 0, may hold values from 1 to 36, 192 in all
- pair_target: int32 [384], P('grp'), parts along dimension 0, may hold values from 0 to 15
Outputs:
- voltage: float32 [32, 64, 1024], P(('grp', 'row'), None, 'col'), parts along dimension 0
There are 2 independent parts, one for each index of `grp`. A program takes and returns all parts, laid end to end along the dimension named above; each array names one. Nothing has to cross between parts.
Inputs may be any that keep to these rules, and one draw needn't show every extreme that they name: `pair_count`: each cluster lists 1 to 36 pairs, 192 in all, and some cluster exactly 36. `geometry`: component 6 (radius) lies in 0.1 to 0.4; positions lie in 0 to 4.
All inputs are finite; a program needn't handle non-finite values.
Results may differ from a plain program's by a relative error of at most 0.0029.
Values may be sent and summed in bfloat16 or wider, within the bound.
No kernel may reach another device: no remote copies, remote signals or barrier semaphores. Data moves between devices by JAX's collectives and lax.ppermute only.
A program may use at most 128 MiB of HBM per device.

v0:
```python
import jax
import jax.numpy as jnp
import numpy as np
from jax import lax
from jax.experimental import pallas as pl
from jax.experimental.pallas import tpu as pltpu
from jax.sharding import PartitionSpec as P

F32 = jnp.float32
BF16 = jnp.bfloat16
NN = (((1,), (0,)), ((), ()))
NT = (((1,), (1,)), ((), ()))
COLS = 64
PACK = 80
VM = pl.BlockSpec(memory_space=pltpu.VMEM)
SM = pl.BlockSpec(memory_space=pltpu.SMEM)
PARAMS = pltpu.CompilerParams(vmem_limit_bytes=44 * 2**20)


def pack_kernel(geometry, currents, packet, block):
    for c in range(geometry.shape[0]):
        g = geometry[c].astype(F32)
        s = g[0:1] * g[0:1] + g[1:2] * g[1:2] + g[2:3] * g[2:3] + g[6:7] * g[6:7]
        s0 = s.astype(BF16).astype(F32)
        s1 = (s - s0).astype(BF16).astype(F32)
        s2 = s - s0 - s1
        one = jnp.ones_like(s)
        rows = jnp.concatenate([g[0:3], one, one, one, s0, s1, s2, g[3:6], jnp.zeros((4, s.shape[1]), F32)], 0)
        rows = rows.astype(BF16)
        packet[c, 0:COLS] = currents[c]
        packet[c, COLS:PACK] = rows
        block[c] = rows


def tiles(sources, weights, offset, left, tangents, acc, d0, d1, k0, k1):
    dist, kern = (d0, d1), (k0, k1)
    nc = left.shape[0]
    for j, source in enumerate(sources):
        nd = source.shape[0]

        def one(d, carry, source=source, base=offset + sum(s.shape[0] for s in sources[:j])):
            rows = source[d, COLS:PACK]
            along = rows.astype(F32)
            for c in range(nc):
                dist[c][...] = lax.dot_general(left[c], rows, NN, preferred_element_type=F32)
            for c in range(nc):
                spread = rows.shape[1] // 128
                coupling = 0.0
                for k in range(3):
                    coupling = coupling + jnp.concatenate([tangents[c, k]] * spread, 1) * along[9 + k : 10 + k]
                kern[c][...] = (coupling * lax.rsqrt(dist[c][...])).astype(BF16)
            for c in range(nc):
                part = lax.dot_general(kern[c][...], source[d, 0:COLS], NT, preferred_element_type=F32)
                acc[c] += weights[c, base + d] * part
            return carry

        lax.fori_loop(0, nd, one, 0)


def first_kernel(packet, other, weights, acc, left, tangents, d0, d1, k0, k1):
    half = other.shape[2]
    for c in range(left.shape[0]):
        for h, rows in enumerate((packet[c, COLS:PACK], other[c])):
            g = rows.astype(F32)
            cells = slice(h * half, (h + 1) * half)
            side = jnp.concatenate([-2.0 * g[0:3], g[6:9], g[3:6], jnp.zeros((7, half), F32)], 0)
            left[c, cells] = side.T.astype(BF16)
            across = jnp.concatenate([g[9:12], jnp.zeros((5, half), F32)], 0).T
            for k in range(3):
                tangents[c, k, cells] = jnp.broadcast_to(across[:, k : k + 1], (half, 128))
    acc[...] = jnp.zeros_like(acc)
    tiles((packet,), weights, 0, left, tangents, acc, d0, d1, k0, k1)


def step_kernel(offset, up, down, weights, left, tangents, acc_in, acc, d0, d1, k0, k1):
    acc[...] = acc_in[...]
    tiles((up, down), weights, offset, left, tangents, acc, d0, d1, k0, k1)


def last_kernel(offset, up, down, weights, left, tangents, acc_in, keep, send, acc, d0, d1, k0, k1):
    acc[...] = acc_in[...]
    tiles((up, down), weights, offset, left, tangents, acc, d0, d1, k0, k1)
    half = keep.shape[2]
    for c in range(keep.shape[0]):
        keep[c] = acc[c, 0:half].T
        send[c] = acc[c, half:].T


def ring_of(n):
    if n == 8:
        return [0, 2, 4, 6, 7, 5, 3, 1]
    return list(range(n))


def body(geometry, currents, pair_count, pair_target):
    nc, _, half = geometry.shape
    n = lax.axis_size("row")
    clusters = pair_count.shape[0]
    shape = jax.ShapeDtypeStruct
    packet, block = pl.pallas_call(
        pack_kernel,
        out_shape=(shape((nc, PACK, half), BF16), shape((nc, 16, half), BF16)),
        in_specs=[VM, VM],
        out_specs=(VM, VM),
    )(geometry, currents)
    other = lax.ppermute(block, "col", [(0, 1), (1, 0)])

    ring = ring_of(n)
    forward = [(ring[i], ring[(i + 1) % n]) for i in range(n)]
    backward = [(b, a) for a, b in forward]
    steps = n // 2
    place = np.argsort(ring)
    order = np.zeros((n, n * nc), np.int32)
    for r in range(n):
        at = [r * nc + i for i in range(nc)]
        for s in range(1, steps + 1):
            before, after = ring[(place[r] - s) % n], ring[(place[r] + s) % n]
            if s < steps:
                at += [before * nc + i for i in range(nc)] + [after * nc + i for i in range(nc)]
            else:
                at += [before * nc + i for i in range(nc)]
        order[r] = at
    row = lax.axis_index("row")
    second = lax.dynamic_slice_in_dim(jnp.asarray(order), row, 1, 0)[0]
    own = row * nc + jnp.arange(nc)
    ends = jnp.sum(jnp.where(np.tri(clusters, dtype=bool), pair_count[None, :], 0), 1)
    first_of = jnp.sum((ends[:, None] <= jnp.arange(pair_target.shape[0])[None, :]).astype(jnp.int32), 0)
    is_a = (first_of[None, None, :] == own[:, None, None]) & (pair_target[None, None, :] == second[None, :, None])
    is_b = (first_of[None, None, :] == second[None, :, None]) & (pair_target[None, None, :] == own[:, None, None])
    weights = jnp.sum(is_a.astype(F32) + is_b.astype(F32), 2)

    cells = 2 * half

    def cost(nd):
        count = nc * nd * cells * half
        return pl.CostEstimate(flops=600 * count, bytes_accessed=1 << 20, transcendentals=count)

    scratch = [pltpu.VMEM((cells, half), F32)] * 2 + [pltpu.VMEM((cells, half), BF16)] * 2
    acc_shape = shape((nc, cells, COLS), F32)
    acc, left, tangents = pl.pallas_call(
        first_kernel,
        out_shape=(acc_shape, shape((nc, cells, 16), BF16), shape((nc, 3, cells, 128), F32)),
        in_specs=[VM, VM, SM],
        out_specs=(VM, VM, VM),
        scratch_shapes=scratch,
        compiler_params=PARAMS,
        cost_estimate=cost(nc),
    )(packet, other, weights)
    def call(kernel, outs, extra, offset, up, down, acc, **kw):
        return pl.pallas_call(
            lambda *refs: kernel(offset, *refs),
            out_shape=outs,
            in_specs=[VM, VM, SM, VM, VM, VM],
            out_specs=jax.tree.map(lambda _: VM, outs),
            scratch_shapes=extra + scratch,
            compiler_params=PARAMS,
            cost_estimate=cost(up.shape[0] + down.shape[0]),
            **kw,
        )(up, down, weights, left, tangents, acc)

    def send_on(s, up, down):
        if s == steps:
            up, down = up[: nc // 2], down[nc // 2 :]
        return lax.ppermute(up, "row", forward), lax.ppermute(down, "row", backward)

    up, down = send_on(1, packet, packet)
    offset = nc
    for s in range(1, steps):
        up, down, acc = lax.optimization_barrier((up, down, acc))
        coming = send_on(s + 1, up, down)
        acc = call(step_kernel, acc_shape, [], offset, up, down, acc, input_output_aliases={5: 0})
        offset += 2 * nc
        up, down = coming
    part = shape((nc, COLS, half), F32)
    keep, send = call(last_kernel, (part, part), [pltpu.VMEM(acc_shape.shape, F32)], offset, up, down, acc)
    return keep + lax.ppermute(send, "col", [(0, 1), (1, 0)])


def solution(mesh):
    placed = (P(("grp", "row"), None, "col"), P(("grp", "row"), None, "col"), P("grp"), P("grp"))
    return jax.shard_map(
        body, mesh=mesh, in_specs=placed, out_specs=P(("grp", "row"), None, "col"), check_vma=False
    )
```

profile of v0, /device:TPU:1, one launch (start us, length us, event | category | flops | bytes accessed | tf_op | source)
XLA Modules:
  0.0 47.0 jit_solution(12617178396212228283)
XLA Ops:
  0.0 1.3 %copy.11.geometry = bf16[2,7,512]{2,1,0:T(8,128)(2,1)} copy(bf16[2,7,512]{2,0,1:T(2,128)(2,1)} %param.6) | data formatting | bytes 28672 | tf_op args[0]
  1.3 1.6 %shard_map.64 = (bf16[2,80,512]{2,1,0:T(8,128)(2,1)}, bf16[2,16,512]{2,1,0:T(8,128)(2,1)}) custom-call(bf16[2,7,512]{2,1,0:T(8,128)(2,1)} %copy.11.geometry, bf16[2,64,512]{2,1,0:T(8,128)(2,1)} %currents.1), custom_call_target="tpu_custom_call" | custom-call | tf_op jit(solution)/shard_map/pallas_call | solution.py:100
  2.9 2.1 %collective-permute-start.1 = (bf16[2,80,512]{2,1,0:T(8,128)(2,1)}, bf16[2,80,512]{2,1,0:T(8,128)(2,1)S(1)}, u32[]{:S(2)}, u32[]{:S(2)}) collective-permute-start(bf16[2,80,512]{2,1,0:T(8,128)(2,1)} %get-tuple-element.21.packet), channel_id=1, source_target_pairs={{4,0},{8,4},{12,8},{14,12},{10,14},{6,10},{2,6},{0,2},{5,1},{9,5},... | collective-permute-start | bytes 491528 | tf_op jit(solution)/shard_map/ppermute | solution.py:164
  5.0 0.1 collective-permute-start
  5.1 1.0 %collective-permute-start.2 = (bf16[2,16,512]{2,1,0:T(8,128)(2,1)}, bf16[2,16,512]{2,1,0:T(8,128)(2,1)S(1)}, u32[]{:S(2)}, u32[]{:S(2)}) collective-permute-start(bf16[2,16,512]{2,1,0:T(8,128)(2,1)} %get-tuple-element.22), channel_id=1, source_target_pairs={{0,1},{1,0},{2,3},{3,2},{4,5},{5,4},{6,7},{7,6},{8,9},{9,8},{10,11... | collective-permute-start | bytes 98312 | tf_op jit(solution)/shard_map/ppermute | solution.py:106
  6.0 0.8 %select_reduce_fusion = s32[16]{0:T(128)S(1)} fusion(pred[16,16]{1,0:T(8,128)(4,1)} %constant.19.clone, s32[16]{0:T(128)} %param.8), kind=kLoop, calls=%fused_computation.5 | loop fusion | flops 496 | bytes 384 | tf_op jit(solution)/shard_map/reduce_sum | solution.py:126
  6.8 0.1 convert_reduce_fusion
  6.9 0.7 %dynamic-slice_bitcast_fusion = s32[16]{0:T(128)S(1)} fusion(s32[8,16]{1,0:T(8,128)} %constant.18.clone, s32[]{:T(128)S(6)} %select_n.8), kind=kLoop, calls=%fused_computation.8 | loop fusion | bytes 132 | tf_op jit(solution)/shard_map/eq | solution.py:128
  7.6 0.8 %broadcast_compare_fusion.3 = (pred[2,192]{1,0:T(4,128)(4,1)S(1)}, pred[2,192]{1,0:T(4,128)(4,1)S(1)}) fusion(s32[192]{0:T(256)S(1)} %convert_reduce_fusion, s32[2]{0:T(128)S(1)} %iota_add_fusion, s32[192]{0:T(256)} %param.9), kind=kLoop, calls=%fused_computation.7 | loop fusion | flops 768 | bytes 2312 | tf_op jit(solution)/shard_map/eq | solution.py:128
  8.4 0.8 %broadcast_compare_fusion.1 = (pred[16,192]{1,0:T(8,128)(4,1)S(1)}, pred[16,192]{1,0:T(8,128)(4,1)S(1)}) fusion(s32[192]{0:T(256)} %param.9, s32[16]{0:T(128)S(1)} %dynamic-slice_bitcast_fusion, s32[192]{0:T(256)S(1)} %convert_reduce_fusion), kind=kLoop, calls=%fused_computation.4 | loop fusion | flops 6144 | bytes 7744 | tf_op jit(solution)/shard_map/eq | solution.py:128
  9.1 0.1 add_reduce_fusion.weights.refs_2_
  9.2 0.0 collective-permute-done.2.other
  9.2 0.0 copy-start
  9.2 0.9 %copy-done = bf16[2,80,512]{2,1,0:T(8,128)(2,1)S(1)} copy-done((bf16[2,80,512]{2,1,0:T(8,128)(2,1)S(1)}, bf16[2,80,512]{2,1,0:T(8,128)(2,1)}, u32[]{:S(2)}) %copy-start) | copy-done | bytes 163864
  10.1 4.3 %shard_map.65 = (f32[2,1024,64]{2,1,0:T(8,128)S(1)}, bf16[2,1024,16]{2,1,0:T(8,128)(2,1)S(1)}, f32[2,3,1024,128]{3,2,1,0:T(8,128)S(1)}) custom-call(bf16[2,80,512]{2,1,0:T(8,128)(2,1)S(1)} %copy-done, bf16[2,16,512]{2,1,0:T(8,128)(2,1)S(1)} %collective-permute-done.2.other, f32[2,16]{1,0:T(2,128)S(1)} %add_reduce_fusion.weights.refs_2_), custom_call_target="tpu_custom_call" | custom-call | flops 1258291200 | bytes 1048576 | tf_op jit(solution)/shard_map/pallas_call | solution.py:140
  14.4 0.0 collective-permute-done.1.refs_1_
  14.4 0.0 collective-permute-done.refs_0_
  14.5 1.8 %collective-permute-start.3 = (bf16[2,80,512]{2,1,0:T(8,128)(2,1)S(1)}, bf16[2,80,512]{2,1,0:T(8,128)(2,1)S(1)}, u32[]{:S(2)}, u32[]{:S(2)}) collective-permute-start(bf16[2,80,512]{2,1,0:T(8,128)(2,1)S(1)} %collective-permute-done.refs_0_), channel_id=1, source_target_pairs={{0,4},{4,8},{8,12},{12,14},{14,10},{10,6},{6,2},{2,0},{1,5},{5,9},... | collective-permute-start | bytes 491528 | tf_op jit(solution)/shard_map/ppermute | solution.py:164
  16.3 0.0 collective-permute-start.4
  16.3 6.7 %shard_map.66.refs_5_ = f32[2,1024,64]{2,1,0:T(8,128)S(1)} custom-call(bf16[2,80,512]{2,1,0:T(8,128)(2,1)S(1)} %collective-permute-done.refs_0_, bf16[2,80,512]{2,1,0:T(8,128)(2,1)S(1)} %collective-permute-done.1.refs_1_, f32[2,16]{1,0:T(2,128)S(1)} %add_reduce_fusion.weights.refs_2_, ...), custom_call_target="tpu_custom_call", output_to_operand_aliasing={{}: (5, {})} | custom-call | flops 2516582400 | bytes 1048576 | tf_op jit(solution)/shard_map/pallas_call | solution.py:150
  23.0 0.0 collective-permute-done.3.refs_0_
  23.0 0.0 collective-permute-done.4.refs_1_
  23.0 1.5 %collective-permute-start.5 = (bf16[2,80,512]{2,1,0:T(8,128)(2,1)S(1)}, bf16[2,80,512]{2,1,0:T(8,128)(2,1)S(1)}, u32[]{:S(2)}, u32[]{:S(2)}) collective-permute-start(bf16[2,80,512]{2,1,0:T(8,128)(2,1)S(1)} %collective-permute-done.3.refs_0_), channel_id=1, source_target_pairs={{0,4},{4,8},{8,12},{12,14},{14,10},{10,6},{6,2},{2,0},{1,5},{5,9},... | collective-permute-start | bytes 491528 | tf_op jit(solution)/shard_map/ppermute | solution.py:164
  24.5 0.0 collective-permute-start.6
  24.5 6.7 %shard_map.67.refs_5_ = f32[2,1024,64]{2,1,0:T(8,128)S(1)} custom-call(bf16[2,80,512]{2,1,0:T(8,128)(2,1)S(1)} %collective-permute-done.3.refs_0_, bf16[2,80,512]{2,1,0:T(8,128)(2,1)S(1)} %collective-permute-done.4.refs_1_, f32[2,16]{1,0:T(2,128)S(1)} %add_reduce_fusion.weights.refs_2_, ...), custom_call_target="tpu_custom_call", output_to_operand_aliasing={{}: (5, {})} | custom-call | flops 2516582400 | bytes 1048576 | tf_op jit(solution)/shard_map/pallas_call | solution.py:150
  31.3 0.0 collective-permute-done.5.refs_0_
  31.3 0.0 collective-permute-done.6.refs_1_
  31.3 1.5 %collective-permute-start.7 = (bf16[1,80,512]{2,1,0:T(8,128)(2,1)S(1)}, bf16[1,80,512]{2,1,0:T(8,128)(2,1)S(1)}, u32[]{:S(2)}, u32[]{:S(2)}) collective-permute-start(bf16[1,80,512]{2,1,0:T(8,128)(2,1)S(1)} %slice.6), channel_id=1, source_target_pairs={{0,4},{4,8},{8,12},{12,14},{14,10},{10,6},{6,2},{2,0},{1,5},{5,9},... | collective-permute-start | bytes 245768 | tf_op jit(solution)/shard_map/ppermute | solution.py:164
  32.8 0.2 collective-permute-start.8
  33.0 6.7 %shard_map.68.refs_5_ = f32[2,1024,64]{2,1,0:T(8,128)S(1)} custom-call(bf16[2,80,512]{2,1,0:T(8,128)(2,1)S(1)} %collective-permute-done.5.refs_0_, bf16[2,80,512]{2,1,0:T(8,128)(2,1)S(1)} %collective-permute-done.6.refs_1_, f32[2,16]{1,0:T(2,128)S(1)} %add_reduce_fusion.weights.refs_2_, ...), custom_call_target="tpu_custom_call", output_to_operand_aliasing={{}: (5, {})} | custom-call | flops 2516582400 | bytes 1048576 | tf_op jit(solution)/shard_map/pallas_call | solution.py:150
  39.7 0.0 collective-permute-done.7.refs_0_
  39.7 0.0 collective-permute-done.8.refs_1_
  39.7 3.9 %shard_map.69 = (f32[2,64,512]{2,1,0:T(8,128)S(1)}, f32[2,64,512]{2,1,0:T(8,128)S(1)}) custom-call(bf16[1,80,512]{2,1,0:T(8,128)(2,1)S(1)} %collective-permute-done.7.refs_0_, bf16[1,80,512]{2,1,0:T(8,128)(2,1)S(1)} %collective-permute-done.8.refs_1_, f32[2,16]{1,0:T(2,128)S(1)} %add_reduce_fusion.weights.refs_2_, ...), custom_call_target="tpu_custom_call" | custom-call | flops 1258291200 | bytes 1048576 | tf_op jit(solution)/shard_map/pallas_call | solution.py:150
  43.6 1.5 %collective-permute-start.9 = (f32[2,64,512]{2,1,0:T(8,128)S(1)}, f32[2,64,512]{2,1,0:T(8,128)S(1)}, u32[]{:S(2)}, u32[]{:S(2)}) collective-permute-start(f32[2,64,512]{2,1,0:T(8,128)S(1)} %get-tuple-element.36), channel_id=1, source_target_pairs={{0,1},{1,0},{2,3},{3,2},{4,5},{5,4},{6,7},{7,6},{8,9},{9,8},{10,11... | collective-permute-start | bytes 786440 | tf_op jit(solution)/shard_map/ppermute | solution.py:176
  45.1 1.2 %collective-permute-done.9 = f32[2,64,512]{2,1,0:T(8,128)S(1)} collective-permute-done((f32[2,64,512]{2,1,0:T(8,128)S(1)}, f32[2,64,512]{2,1,0:T(8,128)S(1)}, u32[]{:S(2)}, u32[]{:S(2)}) %collective-permute-start.9) | collective-permute-done | bytes 262176 | tf_op jit(solution)/shard_map/ppermute | solution.py:176
  46.3 0.7 %add.23 = f32[2,64,512]{2,1,0:T(8,128)} add(f32[2,64,512]{2,1,0:T(8,128)S(1)} %get-tuple-element.35, f32[2,64,512]{2,1,0:T(8,128)S(1)} %collective-permute-done.9) | non-fusion elementwise | flops 65536 | bytes 786432 | tf_op jit(solution)/shard_map/add | solution.py:176
  (3 shorter events, 0.0 us)
Async XLA Ops:
  2.9 11.5 %collective-permute-start.1 = (bf16[2,80,512]{2,1,0:T(8,128)(2,1)}, bf16[2,80,512]{2,1,0:T(8,128)(2,1)S(1)}, u32[]{:S(2)}, u32[]{:S(2)}) collective-permute-start(bf16[2,80,512]{2,1,0:T(8,128)(2,1)} %get-tuple-element.21.packet), channel_id=1, source_target_pairs={{4,0},{8,4},{12,8},{14,12},{10,14},{6,10},{2,6},{0,2},{5,1},{9,5},... | collective-permute-start | bytes 491528 | tf_op jit(solution)/shard_map/ppermute | solution.py:164
  5.0 9.4 %collective-permute-start = (bf16[2,80,512]{2,1,0:T(8,128)(2,1)}, bf16[2,80,512]{2,1,0:T(8,128)(2,1)S(1)}, u32[]{:S(2)}, u32[]{:S(2)}) collective-permute-start(bf16[2,80,512]{2,1,0:T(8,128)(2,1)} %get-tuple-element.21.packet), channel_id=1, source_target_pairs={{0,4},{4,8},{8,12},{12,14},{14,10},{10,6},{6,2},{2,0},{1,5},{5,9},... | collective-permute-start | bytes 491528 | tf_op jit(solution)/shard_map/ppermute | solution.py:164
  5.1 4.2 %collective-permute-start.2 = (bf16[2,16,512]{2,1,0:T(8,128)(2,1)}, bf16[2,16,512]{2,1,0:T(8,128)(2,1)S(1)}, u32[]{:S(2)}, u32[]{:S(2)}) collective-permute-start(bf16[2,16,512]{2,1,0:T(8,128)(2,1)} %get-tuple-element.22), channel_id=1, source_target_pairs={{0,1},{1,0},{2,3},{3,2},{4,5},{5,4},{6,7},{7,6},{8,9},{9,8},{10,11... | collective-permute-start | bytes 98312 | tf_op jit(solution)/shard_map/ppermute | solution.py:106
  9.2 0.9 %copy-start = (bf16[2,80,512]{2,1,0:T(8,128)(2,1)S(1)}, bf16[2,80,512]{2,1,0:T(8,128)(2,1)}, u32[]{:S(2)}) copy-start(bf16[2,80,512]{2,1,0:T(8,128)(2,1)} %get-tuple-element.21.packet) | copy-start | bytes 491524
  14.5 8.5 %collective-permute-start.3 = (bf16[2,80,512]{2,1,0:T(8,128)(2,1)S(1)}, bf16[2,80,512]{2,1,0:T(8,128)(2,1)S(1)}, u32[]{:S(2)}, u32[]{:S(2)}) collective-permute-start(bf16[2,80,512]{2,1,0:T(8,128)(2,1)S(1)} %collective-permute-done.refs_0_), channel_id=1, source_target_pairs={{0,4},{4,8},{8,12},{12,14},{14,10},{10,6},{6,2},{2,0},{1,5},{5,9},... | collective-permute-start | bytes 491528 | tf_op jit(solution)/shard_map/ppermute | solution.py:164
  16.3 6.7 %collective-permute-start.4 = (bf16[2,80,512]{2,1,0:T(8,128)(2,1)S(1)}, bf16[2,80,512]{2,1,0:T(8,128)(2,1)S(1)}, u32[]{:S(2)}, u32[]{:S(2)}) collective-permute-start(bf16[2,80,512]{2,1,0:T(8,128)(2,1)S(1)} %collective-permute-done.1.refs_1_), channel_id=1, source_target_pairs={{4,0},{8,4},{12,8},{14,12},{10,14},{6,10},{2,6},{0,2},{5,1},{9,5},... | collective-permute-start | bytes 491528 | tf_op jit(solution)/shard_map/ppermute | solution.py:164
  23.0 8.3 %collective-permute-start.5 = (bf16[2,80,512]{2,1,0:T(8,128)(2,1)S(1)}, bf16[2,80,512]{2,1,0:T(8,128)(2,1)S(1)}, u32[]{:S(2)}, u32[]{:S(2)}) collective-permute-start(bf16[2,80,512]{2,1,0:T(8,128)(2,1)S(1)} %collective-permute-done.3.refs_0_), channel_id=1, source_target_pairs={{0,4},{4,8},{8,12},{12,14},{14,10},{10,6},{6,2},{2,0},{1,5},{5,9},... | collective-permute-start | bytes 491528 | tf_op jit(solution)/shard_map/ppermute | solution.py:164
  24.5 6.7 %collective-permute-start.6 = (bf16[2,80,512]{2,1,0:T(8,128)(2,1)S(1)}, bf16[2,80,512]{2,1,0:T(8,128)(2,1)S(1)}, u32[]{:S(2)}, u32[]{:S(2)}) collective-permute-start(bf16[2,80,512]{2,1,0:T(8,128)(2,1)S(1)} %collective-permute-done.4.refs_1_), channel_id=1, source_target_pairs={{4,0},{8,4},{12,8},{14,12},{10,14},{6,10},{2,6},{0,2},{5,1},{9,5},... | collective-permute-start | bytes 491528 | tf_op jit(solution)/shard_map/ppermute | solution.py:164
  31.3 8.4 %collective-permute-start.7 = (bf16[1,80,512]{2,1,0:T(8,128)(2,1)S(1)}, bf16[1,80,512]{2,1,0:T(8,128)(2,1)S(1)}, u32[]{:S(2)}, u32[]{:S(2)}) collective-permute-start(bf16[1,80,512]{2,1,0:T(8,128)(2,1)S(1)} %slice.6), channel_id=1, source_target_pairs={{0,4},{4,8},{8,12},{12,14},{14,10},{10,6},{6,2},{2,0},{1,5},{5,9},... | collective-permute-start | bytes 245768 | tf_op jit(solution)/shard_map/ppermute | solution.py:164
  32.8 6.9 %collective-permute-start.8 = (bf16[1,80,512]{2,1,0:T(8,128)(2,1)S(1)}, bf16[1,80,512]{2,1,0:T(8,128)(2,1)S(1)}, u32[]{:S(2)}, u32[]{:S(2)}) collective-permute-start(bf16[1,80,512]{2,1,0:T(8,128)(2,1)S(1)} %slice.7), channel_id=1, source_target_pairs={{4,0},{8,4},{12,8},{14,12},{10,14},{6,10},{2,6},{0,2},{5,1},{9,5},... | collective-permute-start | bytes 245768 | tf_op jit(solution)/shard_map/ppermute | solution.py:164
  43.6 2.6 %collective-permute-start.9 = (f32[2,64,512]{2,1,0:T(8,128)S(1)}, f32[2,64,512]{2,1,0:T(8,128)S(1)}, u32[]{:S(2)}, u32[]{:S(2)}) collective-permute-start(f32[2,64,512]{2,1,0:T(8,128)S(1)} %get-tuple-element.36), channel_id=1, source_target_pairs={{0,1},{1,0},{2,3},{3,2},{4,5},{5,4},{6,7},{7,6},{8,9},{9,8},{10,11... | collective-permute-start | bytes 786440 | tf_op jit(solution)/shard_map/ppermute | solution.py:176
where the time goes:
time: 47.7 us; the launch traced here: 47 us
  Pallas kernels  30 us (63%)
  starting transfers between devices  9.55 us (20%)
  other arithmetic  3.22 us (7%)
  local copies, waits for them, and re-layouts  2.95 us (6%)
  waiting for transfers between devices  1.19 us (2%)
    pallas_call x4, Pallas kernels, call(): pl.pallas_call(lambda *refs: kernel(offset, *refs), out_shape=outs, in_sp...  24.1 us
    ppermute x4, starting transfers between devices, send_on(): lax.ppermute(up, 'row', forward)  4.87 us
    pallas_call x1, Pallas kernels, body(): pl.pallas_call(first_kernel, out_shape=(acc_shape, shape((nc, cells, 16),...  4.29 us
    ppermute x4, starting transfers between devices, send_on(): lax.ppermute(down, 'row', backward)  2.26 us
    unnamed x3, local copies, waits for them, and re-layouts  2.23 us
    pallas_call x1, Pallas kernels, body(): pl.pallas_call(pack_kernel, out_shape=(shape((nc, PACK, half), BF16), sha...  1.63 us
    ppermute x1, starting transfers between devices, body(): return keep + lax.ppermute(send, 'col', [(0, 1), (1, 0)])  1.45 us
    ppermute x1, waiting for transfers between devices, body(): return keep + lax.ppermute(send, 'col', [(0, 1), (1, 0)])  1.16 us
  transfers between devices with their start and end apart: 10, of which 1 were waited for; matrix products, arithmetic and copies ran while one was open for 7% of the time, Pallas kernels for 52%

commit v1 on v0

--- a/solution.py
+++ b/solution.py
@@ -17,37 +17,30 @@
 PARAMS = pltpu.CompilerParams(vmem_limit_bytes=44 * 2**20)
 
 
-def pack_kernel(geometry, currents, packet, block):
-    for c in range(geometry.shape[0]):
-        g = geometry[c].astype(F32)
-        s = g[0:1] * g[0:1] + g[1:2] * g[1:2] + g[2:3] * g[2:3] + g[6:7] * g[6:7]
-        s0 = s.astype(BF16).astype(F32)
-        s1 = (s - s0).astype(BF16).astype(F32)
-        s2 = s - s0 - s1
-        one = jnp.ones_like(s)
-        rows = jnp.concatenate([g[0:3], one, one, one, s0, s1, s2, g[3:6], jnp.zeros((4, s.shape[1]), F32)], 0)
-        rows = rows.astype(BF16)
-        packet[c, 0:COLS] = currents[c]
-        packet[c, COLS:PACK] = rows
-        block[c] = rows
+def squares(g):
+    s = g[0:1] * g[0:1] + g[1:2] * g[1:2] + g[2:3] * g[2:3] + g[6:7] * g[6:7]
+    s0 = s.astype(BF16).astype(F32)
+    s1 = (s - s0).astype(BF16).astype(F32)
+    return [s0, s1, s - s0 - s1]
 
 
 def tiles(sources, weights, offset, left, tangents, acc, d0, d1, k0, k1):
     dist, kern = (d0, d1), (k0, k1)
-    nc = left.shape[0]
+    nc, half = left.shape[0], d0.shape[1]
     for j, source in enumerate(sources):
         nd = source.shape[0]
 
         def one(d, carry, source=source, base=offset + sum(s.shape[0] for s in sources[:j])):
-            rows = source[d, COLS:PACK]
-            along = rows.astype(F32)
+            along = source[d, COLS:PACK].astype(F32)
+            one_row = jnp.ones_like(along[0:1])
+            rows = jnp.concatenate([along[0:3]] + [one_row] * 3 + squares(along) + [jnp.zeros((7, half), F32)], 0)
+            rows = rows.astype(BF16)
             for c in range(nc):
                 dist[c][...] = lax.dot_general(left[c], rows, NN, preferred_element_type=F32)
             for c in range(nc):
-                spread = rows.shape[1] // 128
                 coupling = 0.0
                 for k in range(3):
-                    coupling = coupling + jnp.concatenate([tangents[c, k]] * spread, 1) * along[9 + k : 10 + k]
+                    coupling = coupling + jnp.concatenate([tangents[c, k]] * (half // 128), 1) * along[3 + k : 4 + k]
                 kern[c][...] = (coupling * lax.rsqrt(dist[c][...])).astype(BF16)
             for c in range(nc):
                 part = lax.dot_general(kern[c][...], source[d, 0:COLS], NT, preferred_element_type=F32)
@@ -63,9 +56,10 @@
         for h, rows in enumerate((packet[c, COLS:PACK], other[c])):
             g = rows.astype(F32)
             cells = slice(h * half, (h + 1) * half)
-            side = jnp.concatenate([-2.0 * g[0:3], g[6:9], g[3:6], jnp.zeros((7, half), F32)], 0)
+            one_row = jnp.ones_like(g[0:1])
+            side = jnp.concatenate([-2.0 * g[0:3]] + squares(g) + [one_row] * 3 + [jnp.zeros((7, half), F32)], 0)
             left[c, cells] = side.T.astype(BF16)
-            across = jnp.concatenate([g[9:12], jnp.zeros((5, half), F32)], 0).T
+            across = jnp.concatenate([g[3:6], jnp.zeros((5, half), F32)], 0).T
             for k in range(3):
                 tangents[c, k, cells] = jnp.broadcast_to(across[:, k : k + 1], (half, 128))
     acc[...] = jnp.zeros_like(acc)
@@ -97,32 +91,24 @@
     n = lax.axis_size("row")
     clusters = pair_count.shape[0]
     shape = jax.ShapeDtypeStruct
-    packet, block = pl.pallas_call(
-        pack_kernel,
-        out_shape=(shape((nc, PACK, half), BF16), shape((nc, 16, half), BF16)),
-        in_specs=[VM, VM],
-        out_specs=(VM, VM),
-    )(geometry, currents)
-    other = lax.ppermute(block, "col", [(0, 1), (1, 0)])
+    spare = jnp.zeros((nc, PACK - COLS - geometry.shape[1], half), BF16)
+    packet = jnp.concatenate([currents, geometry, spare], 1)
+    other = lax.ppermute(packet[:, COLS:PACK], "col", [(0, 1), (1, 0)])
 
     ring = ring_of(n)
     forward = [(ring[i], ring[(i + 1) % n]) for i in range(n)]
     backward = [(b, a) for a, b in forward]
     steps = n // 2
-    place = np.argsort(ring)
-    order = np.zeros((n, n * nc), np.int32)
-    for r in range(n):
-        at = [r * nc + i for i in range(nc)]
-        for s in range(1, steps + 1):
-            before, after = ring[(place[r] - s) % n], ring[(place[r] + s) % n]
-            if s < steps:
-                at += [before * nc + i for i in range(nc)] + [after * nc + i for i in range(nc)]
-            else:
-                at += [before * nc + i for i in range(nc)]
-        order[r] = at
     row = lax.axis_index("row")
-    second = lax.dynamic_slice_in_dim(jnp.asarray(order), row, 1, 0)[0]
     own = row * nc + jnp.arange(nc)
+    turn = jnp.arange(n * nc) // nc
+    shift = jnp.where(turn % 2 == 1, -((turn + 1) // 2), turn // 2)
+    if n == 8:
+        spot = (jnp.where(row % 2 == 0, row // 2, n - 1 - row // 2) + shift + n) % n
+        chip = jnp.where(spot < n // 2, 2 * spot, 2 * (n - 1 - spot) + 1)
+    else:
+        chip = (row + shift + n) % n
+    second = chip * nc + jnp.arange(n * nc) % nc
     ends = jnp.sum(jnp.where(np.tri(clusters, dtype=bool), pair_count[None, :], 0), 1)
     first_of = jnp.sum((ends[:, None] <= jnp.arange(pair_target.shape[0])[None, :]).astype(jnp.int32), 0)
     is_a = (first_of[None, None, :] == own[:, None, None]) & (pair_target[None, None, :] == second[None, :, None])

time: 47.7 us -> 45.1 us (0.945)
  local copies, waits for them, and re-layouts: 2.95 us -> 0.82 us
  Pallas kernels: 30 us -> 28.5 us
  other arithmetic: 3.22 us -> 4.25 us
    pallas_call x1 -> x0, Pallas kernels: 1.63 us -> none  [body(): pl.pallas_call(pack_kernel, out_shape=(shape((nc, PACK, half), BF16), sha...]
    unnamed x3 -> x1, local copies, waits for them, and re-layouts: 2.23 us -> 0.72 us
    concatenate x0 -> x1, other arithmetic: none -> 1 us  [body(): packet = jnp.concatenate([currents, geometry, spare], 1)]
    eq x1 -> x0, local copies, waits for them, and re-layouts: 0.7 us -> none  [body(): pair_target[None, None, :] == second[None, :, None]]
  transfers between devices with their start and end apart: 10 -> 10, of which waited for: 1 -> 1; matrix products, arithmetic and copies ran while one was open for 7% -> 6% of each run, Pallas kernels for 52% -> 55%
where the time goes in v1:
time: 45.1 us; the launch traced here: 44.5 us
  Pallas kernels  28.5 us (63%)
  starting transfers between devices  9.65 us (21%)
  other arithmetic  4.25 us (9%)
  waiting for transfers between devices  1.19 us (3%)
  local copies, waits for them, and re-layouts  0.82 us (2%)
    pallas_call x4, Pallas kernels, call(): pl.pallas_call(lambda *refs: kernel(offset, *refs), out_shape=outs, in_sp...  24.1 us
    ppermute x4, starting transfers between devices, send_on(): lax.ppermute(up, 'row', forward)  4.82 us
    pallas_call x1, Pallas kernels, body(): pl.pallas_call(first_kernel, out_shape=(acc_shape, shape((nc, cells, 16),...  4.35 us
    ppermute x4, starting transfers between devices, send_on(): lax.ppermute(down, 'row', backward)  2.38 us
    ppermute x1, starting transfers between devices, body(): return keep + lax.ppermute(send, 'col', [(0, 1), (1, 0)])  1.5 us
    ppermute x1, waiting for transfers between devices, body(): return keep + lax.ppermute(send, 'col', [(0, 1), (1, 0)])  1.16 us
    concatenate x1, other arithmetic, body(): packet = jnp.concatenate([currents, geometry, spare], 1)  1 us
    ppermute x1, starting transfers between devices, body(): other = lax.ppermute(packet[:, COLS:PACK], 'col', [(0, 1), (1, 0)])  0.96 us
  transfers between devices with their start and end apart: 10, of which 1 were waited for; matrix products, arithmetic and copies ran while one was open for 6% of the time, Pallas kernels for 55%

profile of v1, /device:TPU:1, one launch (start us, length us, event | category | flops | bytes accessed | tf_op | source)
XLA Modules:
  0.0 44.5 jit_solution(10821188420797054872)
XLA Ops:
  0.0 0.7 %copy.11 = bf16[2,7,512]{2,1,0:T(8,128)(2,1)S(1)} copy(bf16[2,7,512]{2,0,1:T(2,128)(2,1)} %param.5) | data formatting | bytes 28672 | tf_op args[0]
  0.7 0.1 pad.3.clone
  0.8 1.0 %maximum_maximum_fusion.packet = bf16[2,80,512]{2,1,0:T(8,128)(2,1)S(1)} fusion(bf16[2,7,512]{2,1,0:T(8,128)(2,1)S(1)} %copy.11, bf16[2,64,512]{2,1,0:T(8,128)(2,1)} %param.6, bf16[80]{0:T(256)(128)(2,1)S(1)} %pad.3.clone), kind=kLoop, calls=%fused_computation | loop fusion | flops 491520 | bytes 309408 | tf_op jit(solution)/shard_map/concatenate | solution.py:95
  1.8 2.1 %collective-permute-start.1 = (bf16[2,80,512]{2,1,0:T(8,128)(2,1)S(1)}, bf16[2,80,512]{2,1,0:T(8,128)(2,1)S(1)}, u32[]{:S(2)}, u32[]{:S(2)}) collective-permute-start(bf16[2,80,512]{2,1,0:T(8,128)(2,1)S(1)} %maximum_maximum_fusion.packet), channel_id=1, source_target_pairs={{4,0},{8,4},{12,8},{14,12},{10,14},{6,10},{2,6},{0,2},{5,1},{9,5},... | collective-permute-start | bytes 491528 | tf_op jit(solution)/shard_map/ppermute | solution.py:150
  3.9 0.1 collective-permute-start
  4.0 1.0 %collective-permute-start.2 = (bf16[2,16,512]{2,1,0:T(8,128)(2,1)S(1)}, bf16[2,16,512]{2,1,0:T(8,128)(2,1)S(1)}, u32[]{:S(2)}, u32[]{:S(2)}) collective-permute-start(bf16[2,16,512]{2,1,0:T(8,128)(2,1)S(1)} %concatenate.7), channel_id=1, source_target_pairs={{0,1},{1,0},{2,3},{3,2},{4,5},{5,4},{6,7},{7,6},{8,9},{9,8},{10,11... | collective-permute-start | bytes 98312 | tf_op jit(solution)/shard_map/ppermute | solution.py:96
  5.0 0.8 %select_reduce_fusion = s32[16]{0:T(128)S(1)} fusion(pred[16,16]{1,0:T(8,128)(4,1)} %constant.96.clone, s32[16]{0:T(128)} %param.7), kind=kLoop, calls=%fused_computation.6 | loop fusion | flops 496 | bytes 384 | tf_op jit(solution)/shard_map/reduce_sum | solution.py:112
  5.8 0.1 convert_reduce_fusion
  5.9 0.8 %broadcast_compare_fusion.3 = (pred[2,192]{1,0:T(4,128)(4,1)S(1)}, pred[2,192]{1,0:T(4,128)(4,1)S(1)}) fusion(s32[192]{0:T(256)S(1)} %convert_reduce_fusion, s32[2]{0:T(128)S(1)} %iota_add_fusion, s32[192]{0:T(256)} %param.8), kind=kLoop, calls=%fused_computation.27 | loop fusion | flops 768 | bytes 2312 | tf_op jit(solution)/shard_map/eq | solution.py:114
  6.7 0.8 %broadcast_compare_fusion.1 = (pred[16,192]{1,0:T(8,128)(4,1)S(1)}, pred[16,192]{1,0:T(8,128)(4,1)S(1)}) fusion(s32[192]{0:T(256)} %param.8, s32[16]{0:T(128)S(1)} %fusion, s32[192]{0:T(256)S(1)} %convert_reduce_fusion), kind=kLoop, calls=%fused_computation.5 | loop fusion | flops 6144 | bytes 7744 | tf_op jit(solution)/shard_map/eq | solution.py:114
  7.4 0.1 add_reduce_fusion.weights.refs_2_
  7.5 0.0 collective-permute-done.2.other
  7.5 4.4 %shard_map.55 = (f32[2,1024,64]{2,1,0:T(8,128)S(1)}, bf16[2,1024,16]{2,1,0:T(8,128)(2,1)S(1)}, f32[2,3,1024,128]{3,2,1,0:T(8,128)S(1)}) custom-call(bf16[2,80,512]{2,1,0:T(8,128)(2,1)S(1)} %maximum_maximum_fusion.packet, bf16[2,16,512]{2,1,0:T(8,128)(2,1)S(1)} %collective-permute-done.2.other, f32[2,16]{1,0:T(2,128)S(1)} %add_reduce_fusion.weights.refs_2_), custom_call_target="tpu_custom_call" | custom-call | flops 1258291200 | bytes 1048576 | tf_op jit(solution)/shard_map/pallas_call | solution.py:126
  11.9 0.0 collective-permute-done.1.refs_1_
  11.9 0.0 collective-permute-done.refs_0_
  11.9 1.7 %collective-permute-start.3 = (bf16[2,80,512]{2,1,0:T(8,128)(2,1)S(1)}, bf16[2,80,512]{2,1,0:T(8,128)(2,1)S(1)}, u32[]{:S(2)}, u32[]{:S(2)}) collective-permute-start(bf16[2,80,512]{2,1,0:T(8,128)(2,1)S(1)} %collective-permute-done.refs_0_), channel_id=1, source_target_pairs={{0,4},{4,8},{8,12},{12,14},{14,10},{10,6},{6,2},{2,0},{1,5},{5,9},... | collective-permute-start | bytes 491528 | tf_op jit(solution)/shard_map/ppermute | solution.py:150
  13.7 0.0 collective-permute-start.4
  13.7 6.7 %shard_map.56.refs_5_ = f32[2,1024,64]{2,1,0:T(8,128)S(1)} custom-call(bf16[2,80,512]{2,1,0:T(8,128)(2,1)S(1)} %collective-permute-done.refs_0_, bf16[2,80,512]{2,1,0:T(8,128)(2,1)S(1)} %collective-permute-done.1.refs_1_, f32[2,16]{1,0:T(2,128)S(1)} %add_reduce_fusion.weights.refs_2_, ...), custom_call_target="tpu_custom_call", output_to_operand_aliasing={{}: (5, {})} | custom-call | flops 2516582400 | bytes 1048576 | tf_op jit(solution)/shard_map/pallas_call | solution.py:136
  20.4 0.0 collective-permute-done.3.refs_0_
  20.4 0.0 collective-permute-done.4.refs_1_
  20.5 1.5 %collective-permute-start.5 = (bf16[2,80,512]{2,1,0:T(8,128)(2,1)S(1)}, bf16[2,80,512]{2,1,0:T(8,128)(2,1)S(1)}, u32[]{:S(2)}, u32[]{:S(2)}) collective-permute-start(bf16[2,80,512]{2,1,0:T(8,128)(2,1)S(1)} %collective-permute-done.3.refs_0_), channel_id=1, source_target_pairs={{0,4},{4,8},{8,12},{12,14},{14,10},{10,6},{6,2},{2,0},{1,5},{5,9},... | collective-permute-start | bytes 491528 | tf_op jit(solution)/shard_map/ppermute | solution.py:150
  21.9 0.0 collective-permute-start.6
  22.0 6.7 %shard_map.57.refs_5_ = f32[2,1024,64]{2,1,0:T(8,128)S(1)} custom-call(bf16[2,80,512]{2,1,0:T(8,128)(2,1)S(1)} %collective-permute-done.3.refs_0_, bf16[2,80,512]{2,1,0:T(8,128)(2,1)S(1)} %collective-permute-done.4.refs_1_, f32[2,16]{1,0:T(2,128)S(1)} %add_reduce_fusion.weights.refs_2_, ...), custom_call_target="tpu_custom_call", output_to_operand_aliasing={{}: (5, {})} | custom-call | flops 2516582400 | bytes 1048576 | tf_op jit(solution)/shard_map/pallas_call | solution.py:136
  28.7 0.0 collective-permute-done.5.refs_0_
  28.7 0.0 collective-permute-done.6.refs_1_
  28.8 1.5 %collective-permute-start.7 = (bf16[1,80,512]{2,1,0:T(8,128)(2,1)S(1)}, bf16[1,80,512]{2,1,0:T(8,128)(2,1)S(1)}, u32[]{:S(2)}, u32[]{:S(2)}) collective-permute-start(bf16[1,80,512]{2,1,0:T(8,128)(2,1)S(1)} %slice.8), channel_id=1, source_target_pairs={{0,4},{4,8},{8,12},{12,14},{14,10},{10,6},{6,2},{2,0},{1,5},{5,9},... | collective-permute-start | bytes 245768 | tf_op jit(solution)/shard_map/ppermute | solution.py:150
  30.3 0.2 collective-permute-start.8
  30.4 6.7 %shard_map.58.refs_5_ = f32[2,1024,64]{2,1,0:T(8,128)S(1)} custom-call(bf16[2,80,512]{2,1,0:T(8,128)(2,1)S(1)} %collective-permute-done.5.refs_0_, bf16[2,80,512]{2,1,0:T(8,128)(2,1)S(1)} %collective-permute-done.6.refs_1_, f32[2,16]{1,0:T(2,128)S(1)} %add_reduce_fusion.weights.refs_2_, ...), custom_call_target="tpu_custom_call", output_to_operand_aliasing={{}: (5, {})} | custom-call | flops 2516582400 | bytes 1048576 | tf_op jit(solution)/shard_map/pallas_call | solution.py:136
  37.2 0.0 collective-permute-done.7.refs_0_
  37.2 0.0 collective-permute-done.8.refs_1_
  37.2 3.9 %shard_map.59 = (f32[2,64,512]{2,1,0:T(8,128)S(1)}, f32[2,64,512]{2,1,0:T(8,128)S(1)}) custom-call(bf16[1,80,512]{2,1,0:T(8,128)(2,1)S(1)} %collective-permute-done.7.refs_0_, bf16[1,80,512]{2,1,0:T(8,128)(2,1)S(1)} %collective-permute-done.8.refs_1_, f32[2,16]{1,0:T(2,128)S(1)} %add_reduce_fusion.weights.refs_2_, ...), custom_call_target="tpu_custom_call" | custom-call | flops 1258291200 | bytes 1048576 | tf_op jit(solution)/shard_map/pallas_call | solution.py:136
  41.1 1.5 %collective-permute-start.9 = (f32[2,64,512]{2,1,0:T(8,128)S(1)}, f32[2,64,512]{2,1,0:T(8,128)S(1)}, u32[]{:S(2)}, u32[]{:S(2)}) collective-permute-start(f32[2,64,512]{2,1,0:T(8,128)S(1)} %get-tuple-element.32), channel_id=1, source_target_pairs={{0,1},{1,0},{2,3},{3,2},{4,5},{5,4},{6,7},{7,6},{8,9},{9,8},{10,11... | collective-permute-start | bytes 786440 | tf_op jit(solution)/shard_map/ppermute | solution.py:162
  42.6 1.2 %collective-permute-done.9 = f32[2,64,512]{2,1,0:T(8,128)S(1)} collective-permute-done((f32[2,64,512]{2,1,0:T(8,128)S(1)}, f32[2,64,512]{2,1,0:T(8,128)S(1)}, u32[]{:S(2)}, u32[]{:S(2)}) %collective-permute-start.9) | collective-permute-done | bytes 262176 | tf_op jit(solution)/shard_map/ppermute | solution.py:162
  43.8 0.7 %add.115 = f32[2,64,512]{2,1,0:T(8,128)} add(f32[2,64,512]{2,1,0:T(8,128)S(1)} %get-tuple-element.31, f32[2,64,512]{2,1,0:T(8,128)S(1)} %collective-permute-done.9) | non-fusion elementwise | flops 65536 | bytes 786432 | tf_op jit(solution)/shard_map/add | solution.py:162
  (6 shorter events, 0.0 us)
Async XLA Ops:
  1.8 10.1 %collective-permute-start.1 = (bf16[2,80,512]{2,1,0:T(8,128)(2,1)S(1)}, bf16[2,80,512]{2,1,0:T(8,128)(2,1)S(1)}, u32[]{:S(2)}, u32[]{:S(2)}) collective-permute-start(bf16[2,80,512]{2,1,0:T(8,128)(2,1)S(1)} %maximum_maximum_fusion.packet), channel_id=1, source_target_pairs={{4,0},{8,4},{12,8},{14,12},{10,14},{6,10},{2,6},{0,2},{5,1},{9,5},... | collective-permute-start | bytes 491528 | tf_op jit(solution)/shard_map/ppermute | solution.py:150
  3.9 8.0 %collective-permute-start = (bf16[2,80,512]{2,1,0:T(8,128)(2,1)S(1)}, bf16[2,80,512]{2,1,0:T(8,128)(2,1)S(1)}, u32[]{:S(2)}, u32[]{:S(2)}) collective-permute-start(bf16[2,80,512]{2,1,0:T(8,128)(2,1)S(1)} %maximum_maximum_fusion.packet), channel_id=1, source_target_pairs={{0,4},{4,8},{8,12},{12,14},{14,10},{10,6},{6,2},{2,0},{1,5},{5,9},... | collective-permute-start | bytes 491528 | tf_op jit(solution)/shard_map/ppermute | solution.py:150
  4.0 3.5 %collective-permute-start.2 = (bf16[2,16,512]{2,1,0:T(8,128)(2,1)S(1)}, bf16[2,16,512]{2,1,0:T(8,128)(2,1)S(1)}, u32[]{:S(2)}, u32[]{:S(2)}) collective-permute-start(bf16[2,16,512]{2,1,0:T(8,128)(2,1)S(1)} %concatenate.7), channel_id=1, source_target_pairs={{0,1},{1,0},{2,3},{3,2},{4,5},{5,4},{6,7},{7,6},{8,9},{9,8},{10,11... | collective-permute-start | bytes 98312 | tf_op jit(solution)/shard_map/ppermute | solution.py:96
  11.9 8.5 %collective-permute-start.3 = (bf16[2,80,512]{2,1,0:T(8,128)(2,1)S(1)}, bf16[2,80,512]{2,1,0:T(8,128)(2,1)S(1)}, u32[]{:S(2)}, u32[]{:S(2)}) collective-permute-start(bf16[2,80,512]{2,1,0:T(8,128)(2,1)S(1)} %collective-permute-done.refs_0_), channel_id=1, source_target_pairs={{0,4},{4,8},{8,12},{12,14},{14,10},{10,6},{6,2},{2,0},{1,5},{5,9},... | collective-permute-start | bytes 491528 | tf_op jit(solution)/shard_map/ppermute | solution.py:150
  13.7 6.8 %collective-permute-start.4 = (bf16[2,80,512]{2,1,0:T(8,128)(2,1)S(1)}, bf16[2,80,512]{2,1,0:T(8,128)(2,1)S(1)}, u32[]{:S(2)}, u32[]{:S(2)}) collective-permute-start(bf16[2,80,512]{2,1,0:T(8,128)(2,1)S(1)} %collective-permute-done.1.refs_1_), channel_id=1, source_target_pairs={{4,0},{8,4},{12,8},{14,12},{10,14},{6,10},{2,6},{0,2},{5,1},{9,5},... | collective-permute-start | bytes 491528 | tf_op jit(solution)/shard_map/ppermute | solution.py:150
  20.5 8.3 %collective-permute-start.5 = (bf16[2,80,512]{2,1,0:T(8,128)(2,1)S(1)}, bf16[2,80,512]{2,1,0:T(8,128)(2,1)S(1)}, u32[]{:S(2)}, u32[]{:S(2)}) collective-permute-start(bf16[2,80,512]{2,1,0:T(8,128)(2,1)S(1)} %collective-permute-done.3.refs_0_), channel_id=1, source_target_pairs={{0,4},{4,8},{8,12},{12,14},{14,10},{10,6},{6,2},{2,0},{1,5},{5,9},... | collective-permute-start | bytes 491528 | tf_op jit(solution)/shard_map/ppermute | solution.py:150
  21.9 6.8 %collective-permute-start.6 = (bf16[2,80,512]{2,1,0:T(8,128)(2,1)S(1)}, bf16[2,80,512]{2,1,0:T(8,128)(2,1)S(1)}, u32[]{:S(2)}, u32[]{:S(2)}) collective-permute-start(bf16[2,80,512]{2,1,0:T(8,128)(2,1)S(1)} %collective-permute-done.4.refs_1_), channel_id=1, source_target_pairs={{4,0},{8,4},{12,8},{14,12},{10,14},{6,10},{2,6},{0,2},{5,1},{9,5},... | collective-permute-start | bytes 491528 | tf_op jit(solution)/shard_map/ppermute | solution.py:150
  28.8 8.4 %collective-permute-start.7 = (bf16[1,80,512]{2,1,0:T(8,128)(2,1)S(1)}, bf16[1,80,512]{2,1,0:T(8,128)(2,1)S(1)}, u32[]{:S(2)}, u32[]{:S(2)}) collective-permute-start(bf16[1,80,512]{2,1,0:T(8,128)(2,1)S(1)} %slice.8), channel_id=1, source_target_pairs={{0,4},{4,8},{8,12},{12,14},{14,10},{10,6},{6,2},{2,0},{1,5},{5,9},... | collective-permute-start | bytes 245768 | tf_op jit(solution)/shard_map/ppermute | solution.py:150
  30.3 7.0 %collective-permute-start.8 = (bf16[1,80,512]{2,1,0:T(8,128)(2,1)S(1)}, bf16[1,80,512]{2,1,0:T(8,128)(2,1)S(1)}, u32[]{:S(2)}, u32[]{:S(2)}) collective-permute-start(bf16[1,80,512]{2,1,0:T(8,128)(2,1)S(1)} %slice.9), channel_id=1, source_target_pairs={{4,0},{8,4},{12,8},{14,12},{10,14},{6,10},{2,6},{0,2},{5,1},{9,5},... | collective-permute-start | bytes 245768 | tf_op jit(solution)/shard_map/ppermute | solution.py:150
  41.1 2.7 %collective-permute-start.9 = (f32[2,64,512]{2,1,0:T(8,128)S(1)}, f32[2,64,512]{2,1,0:T(8,128)S(1)}, u32[]{:S(2)}, u32[]{:S(2)}) collective-permute-start(f32[2,64,512]{2,1,0:T(8,128)S(1)} %get-tuple-element.32), channel_id=1, source_target_pairs={{0,1},{1,0},{2,3},{3,2},{4,5},{5,4},{6,7},{7,6},{8,9},{9,8},{10,11... | collective-permute-start | bytes 786440 | tf_op jit(solution)/shard_map/ppermute | solution.py:162

commit v2 on v1

--- a/solution.py
+++ b/solution.py
@@ -13,7 +13,6 @@
 COLS = 64
 PACK = 80
 VM = pl.BlockSpec(memory_space=pltpu.VMEM)
-SM = pl.BlockSpec(memory_space=pltpu.SMEM)
 PARAMS = pltpu.CompilerParams(vmem_limit_bytes=44 * 2**20)
 
 
@@ -44,7 +43,7 @@
                 kern[c][...] = (coupling * lax.rsqrt(dist[c][...])).astype(BF16)
             for c in range(nc):
                 part = lax.dot_general(kern[c][...], source[d, 0:COLS], NT, preferred_element_type=F32)
-                acc[c] += weights[c, base + d] * part
+                acc[c] += weights[c, pl.ds(base + d, 1)] * part
             return carry
 
         lax.fori_loop(0, nd, one, 0)
@@ -111,9 +110,11 @@
     second = chip * nc + jnp.arange(n * nc) % nc
     ends = jnp.sum(jnp.where(np.tri(clusters, dtype=bool), pair_count[None, :], 0), 1)
     first_of = jnp.sum((ends[:, None] <= jnp.arange(pair_target.shape[0])[None, :]).astype(jnp.int32), 0)
-    is_a = (first_of[None, None, :] == own[:, None, None]) & (pair_target[None, None, :] == second[None, :, None])
-    is_b = (first_of[None, None, :] == second[None, :, None]) & (pair_target[None, None, :] == own[:, None, None])
-    weights = jnp.sum(is_a.astype(F32) + is_b.astype(F32), 2)
+    listed = first_of * clusters + pair_target
+    turned = pair_target * clusters + first_of
+    wanted = (own[:, None] * clusters + second[None, :])[:, :, None]
+    times = jnp.sum((listed == wanted).astype(F32) + (turned == wanted).astype(F32), 2)
+    weights = jnp.broadcast_to(times[:, :, None], (nc, n * nc, COLS))
 
     cells = 2 * half
 
@@ -126,7 +127,7 @@
     acc, left, tangents = pl.pallas_call(
         first_kernel,
         out_shape=(acc_shape, shape((nc, cells, 16), BF16), shape((nc, 3, cells, 128), F32)),
-        in_specs=[VM, VM, SM],
+        in_specs=[VM, VM, VM],
         out_specs=(VM, VM, VM),
         scratch_shapes=scratch,
         compiler_params=PARAMS,
@@ -136,7 +137,7 @@
         return pl.pallas_call(
             lambda *refs: kernel(offset, *refs),
             out_shape=outs,
-            in_specs=[VM, VM, SM, VM, VM, VM],
+            in_specs=[VM] * 6,
             out_specs=jax.tree.map(lambda _: VM, outs),
             scratch_shapes=extra + scratch,
             compiler_params=PARAMS,

time: 45.1 us -> 39.9 us (0.88)
  Pallas kernels: 28.5 us -> 23.5 us
  other arithmetic: 4.25 us -> 3.57 us
    pallas_call x4, Pallas kernels: 24.1 us -> 20 us  [call(): pl.pallas_call(lambda *refs: kernel(offset, *refs), out_shape=outs, in_sp...]
    eq x2 -> x0, other arithmetic: 1.51 us -> none  [the longest x1 0.75 us: body(): first_of[None, None, :] == own[:, None, None]]
    pallas_call x1, Pallas kernels: 4.35 us -> 3.52 us  [body(): pl.pallas_call(first_kernel, out_shape=(acc_shape, shape((nc, cells, 16),...]
    add x1 -> x2, other arithmetic: 0.01 us -> 0.75 us  [the longest x1 0.68 us: body(): listed = first_of * clusters + pair_target]
  transfers between devices with their start and end apart: 10 -> 10, of which waited for: 1 -> 1; matrix products, arithmetic and copies ran while one was open for 6% -> 5% of each run, Pallas kernels for 55% -> 52%
where the time goes in v2:
time: 39.9 us; the launch traced here: 39.3 us
  Pallas kernels  23.5 us (59%)
  starting transfers between devices  10 us (25%)
  other arithmetic  3.57 us (9%)
  waiting for transfers between devices  1.19 us (3%)
  local copies, waits for them, and re-layouts  0.89 us (2%)
    pallas_call x4, Pallas kernels, call(): pl.pallas_call(lambda *refs: kernel(offset, *refs), out_shape=outs, in_sp...  20 us
    ppermute x4, starting transfers between devices, send_on(): lax.ppermute(up, 'row', forward)  4.83 us
    pallas_call x1, Pallas kernels, body(): pl.pallas_call(first_kernel, out_shape=(acc_shape, shape((nc, cells, 16),...  3.52 us
    ppermute x4, starting transfers between devices, send_on(): lax.ppermute(down, 'row', backward)  2.37 us
    ppermute x1, starting transfers between devices, body(): return keep + lax.ppermute(send, 'col', [(0, 1), (1, 0)])  1.85 us
    ppermute x1, waiting for transfers between devices, body(): return keep + lax.ppermute(send, 'col', [(0, 1), (1, 0)])  1.16 us
    concatenate x1, other arithmetic, body(): packet = jnp.concatenate([currents, geometry, spare], 1)  1 us
    ppermute x1, starting transfers between devices, body(): other = lax.ppermute(packet[:, COLS:PACK], 'col', [(0, 1), (1, 0)])  0.96 us
  transfers between devices with their start and end apart: 10, of which 1 were waited for; matrix products, arithmetic and copies ran while one was open for 5% of the time, Pallas kernels for 52%

profile of v2, /device:TPU:1, one launch (start us, length us, event | category | flops | bytes accessed | tf_op | source)
XLA Modules:
  0.0 39.3 jit_solution(13852102262162859920)
XLA Ops:
  0.0 0.7 %copy.11 = bf16[2,7,512]{2,1,0:T(8,128)(2,1)S(1)} copy(bf16[2,7,512]{2,0,1:T(2,128)(2,1)} %param.5) | data formatting | bytes 28672 | tf_op args[0]
  0.7 0.1 pad.3.clone
  0.8 1.0 %maximum_maximum_fusion.packet = bf16[2,80,512]{2,1,0:T(8,128)(2,1)S(1)} fusion(bf16[2,7,512]{2,1,0:T(8,128)(2,1)S(1)} %copy.11, bf16[2,64,512]{2,1,0:T(8,128)(2,1)} %param.6, bf16[80]{0:T(256)(128)(2,1)S(1)} %pad.3.clone), kind=kLoop, calls=%fused_computation | loop fusion | flops 491520 | bytes 309408 | tf_op jit(solution)/shard_map/concatenate | solution.py:94
  1.8 2.1 %collective-permute-start.1 = (bf16[2,80,512]{2,1,0:T(8,128)(2,1)S(1)}, bf16[2,80,512]{2,1,0:T(8,128)(2,1)S(1)}, u32[]{:S(2)}, u32[]{:S(2)}) collective-permute-start(bf16[2,80,512]{2,1,0:T(8,128)(2,1)S(1)} %maximum_maximum_fusion.packet), channel_id=1, source_target_pairs={{4,0},{8,4},{12,8},{14,12},{10,14},{6,10},{2,6},{0,2},{5,1},{9,5},... | collective-permute-start | bytes 491528 | tf_op jit(solution)/shard_map/ppermute | solution.py:151
  3.9 0.1 collective-permute-start
  4.0 1.0 %collective-permute-start.2 = (bf16[2,16,512]{2,1,0:T(8,128)(2,1)S(1)}, bf16[2,16,512]{2,1,0:T(8,128)(2,1)S(1)}, u32[]{:S(2)}, u32[]{:S(2)}) collective-permute-start(bf16[2,16,512]{2,1,0:T(8,128)(2,1)S(1)} %concatenate.7), channel_id=1, source_target_pairs={{0,1},{1,0},{2,3},{3,2},{4,5},{5,4},{6,7},{7,6},{8,9},{9,8},{10,11... | collective-permute-start | bytes 98312 | tf_op jit(solution)/shard_map/ppermute | solution.py:95
  5.0 0.8 %select_reduce_fusion = s32[16]{0:T(128)S(1)} fusion(pred[16,16]{1,0:T(8,128)(4,1)} %constant.99.clone, s32[16]{0:T(128)} %param.7), kind=kLoop, calls=%fused_computation.4 | loop fusion | flops 496 | bytes 384 | tf_op jit(solution)/shard_map/reduce_sum | solution.py:111
  5.8 0.1 convert_reduce_fusion
  5.9 0.1 broadcast_add_fusion
  6.0 0.7 %multiply_add_fusion.1 = (s32[192]{0:T(256)S(1)}, s32[192]{0:T(256)S(1)}) fusion(s32[192]{0:T(256)} %param.8, s32[192]{0:T(256)S(1)} %convert_reduce_fusion), kind=kLoop, calls=%fused_computation.25 | loop fusion | flops 768 | bytes 3072 | tf_op jit(solution)/shard_map/add | solution.py:113
  6.7 0.2 add_reduce_fusion
  6.8 0.0 collective-permute-done.2.other
  6.9 0.1 broadcast_in_dim.19.weights.refs_2_
  6.9 3.5 %shard_map.55 = (f32[2,1024,64]{2,1,0:T(8,128)S(1)}, bf16[2,1024,16]{2,1,0:T(8,128)(2,1)S(1)}, f32[2,3,1024,128]{3,2,1,0:T(8,128)S(1)}) custom-call(bf16[2,80,512]{2,1,0:T(8,128)(2,1)S(1)} %maximum_maximum_fusion.packet, bf16[2,16,512]{2,1,0:T(8,128)(2,1)S(1)} %collective-permute-done.2.other, f32[2,16,64]{2,1,0:T(8,128)S(1)} %broadcast_in_dim.19.weights.refs_2_), custom_call_target="tpu_custom_call" | custom-call | flops 1258291200 | bytes 1048576 | tf_op jit(solution)/shard_map/pallas_call | solution.py:127
  10.5 0.0 collective-permute-done.1.refs_1_
  10.5 0.0 collective-permute-done.refs_0_
  10.5 1.7 %collective-permute-start.3 = (bf16[2,80,512]{2,1,0:T(8,128)(2,1)S(1)}, bf16[2,80,512]{2,1,0:T(8,128)(2,1)S(1)}, u32[]{:S(2)}, u32[]{:S(2)}) collective-permute-start(bf16[2,80,512]{2,1,0:T(8,128)(2,1)S(1)} %collective-permute-done.refs_0_), channel_id=1, source_target_pairs={{0,4},{4,8},{8,12},{12,14},{14,10},{10,6},{6,2},{2,0},{1,5},{5,9},... | collective-permute-start | bytes 491528 | tf_op jit(solution)/shard_map/ppermute | solution.py:151
  12.2 0.0 collective-permute-start.4
  12.2 5.7 %shard_map.56.refs_5_ = f32[2,1024,64]{2,1,0:T(8,128)S(1)} custom-call(bf16[2,80,512]{2,1,0:T(8,128)(2,1)S(1)} %collective-permute-done.refs_0_, bf16[2,80,512]{2,1,0:T(8,128)(2,1)S(1)} %collective-permute-done.1.refs_1_, f32[2,16,64]{2,1,0:T(8,128)S(1)} %broadcast_in_dim.19.weights.refs_2_, ...), custom_call_target="tpu_custom_call", output_to_operand_aliasing={{}: (5, {})} | custom-call | flops 2516582400 | bytes 1048576 | tf_op jit(solution)/shard_map/pallas_call | solution.py:137
  17.9 0.0 collective-permute-done.3.refs_0_
  17.9 0.0 collective-permute-done.4.refs_1_
  17.9 1.5 %collective-permute-start.5 = (bf16[2,80,512]{2,1,0:T(8,128)(2,1)S(1)}, bf16[2,80,512]{2,1,0:T(8,128)(2,1)S(1)}, u32[]{:S(2)}, u32[]{:S(2)}) collective-permute-start(bf16[2,80,512]{2,1,0:T(8,128)(2,1)S(1)} %collective-permute-done.3.refs_0_), channel_id=1, source_target_pairs={{0,4},{4,8},{8,12},{12,14},{14,10},{10,6},{6,2},{2,0},{1,5},{5,9},... | collective-permute-start | bytes 491528 | tf_op jit(solution)/shard_map/ppermute | solution.py:151
  19.4 0.0 collective-permute-start.6
  19.4 5.7 %shard_map.57.refs_5_ = f32[2,1024,64]{2,1,0:T(8,128)S(1)} custom-call(bf16[2,80,512]{2,1,0:T(8,128)(2,1)S(1)} %collective-permute-done.3.refs_0_, bf16[2,80,512]{2,1,0:T(8,128)(2,1)S(1)} %collective-permute-done.4.refs_1_, f32[2,16,64]{2,1,0:T(8,128)S(1)} %broadcast_in_dim.19.weights.refs_2_, ...), custom_call_target="tpu_custom_call", output_to_operand_aliasing={{}: (5, {})} | custom-call | flops 2516582400 | bytes 1048576 | tf_op jit(solution)/shard_map/pallas_call | solution.py:137
  25.1 0.0 collective-permute-done.5.refs_0_
  25.1 0.0 collective-permute-done.6.refs_1_
  25.2 1.5 %collective-permute-start.7 = (bf16[1,80,512]{2,1,0:T(8,128)(2,1)S(1)}, bf16[1,80,512]{2,1,0:T(8,128)(2,1)S(1)}, u32[]{:S(2)}, u32[]{:S(2)}) collective-permute-start(bf16[1,80,512]{2,1,0:T(8,128)(2,1)S(1)} %slice.8), channel_id=1, source_target_pairs={{0,4},{4,8},{8,12},{12,14},{14,10},{10,6},{6,2},{2,0},{1,5},{5,9},... | collective-permute-start | bytes 245768 | tf_op jit(solution)/shard_map/ppermute | solution.py:151
  26.7 0.2 collective-permute-start.8
  26.8 5.7 %shard_map.58.refs_5_ = f32[2,1024,64]{2,1,0:T(8,128)S(1)} custom-call(bf16[2,80,512]{2,1,0:T(8,128)(2,1)S(1)} %collective-permute-done.5.refs_0_, bf16[2,80,512]{2,1,0:T(8,128)(2,1)S(1)} %collective-permute-done.6.refs_1_, f32[2,16,64]{2,1,0:T(8,128)S(1)} %broadcast_in_dim.19.weights.refs_2_, ...), custom_call_target="tpu_custom_call", output_to_operand_aliasing={{}: (5, {})} | custom-call | flops 2516582400 | bytes 1048576 | tf_op jit(solution)/shard_map/pallas_call | solution.py:137
  32.5 0.0 collective-permute-done.7.refs_0_
  32.5 0.0 collective-permute-done.8.refs_1_
  32.5 3.0 %shard_map.59 = (f32[2,64,512]{2,1,0:T(8,128)S(1)}, f32[2,64,512]{2,1,0:T(8,128)S(1)}) custom-call(bf16[1,80,512]{2,1,0:T(8,128)(2,1)S(1)} %collective-permute-done.7.refs_0_, bf16[1,80,512]{2,1,0:T(8,128)(2,1)S(1)} %collective-permute-done.8.refs_1_, f32[2,16,64]{2,1,0:T(8,128)S(1)} %broadcast_in_dim.19.weights.refs_2_, ...), custom_call_target="tpu_custom_call" | custom-call | flops 1258291200 | bytes 1048576 | tf_op jit(solution)/shard_map/pallas_call | solution.py:137
  35.6 1.8 %collective-permute-start.9 = (f32[2,64,512]{2,1,0:T(8,128)S(1)}, f32[2,64,512]{2,1,0:T(8,128)S(1)}, u32[]{:S(2)}, u32[]{:S(2)}) collective-permute-start(f32[2,64,512]{2,1,0:T(8,128)S(1)} %get-tuple-element.32), channel_id=1, source_target_pairs={{0,1},{1,0},{2,3},{3,2},{4,5},{5,4},{6,7},{7,6},{8,9},{9,8},{10,11... | collective-permute-start | bytes 786440 | tf_op jit(solution)/shard_map/ppermute | solution.py:163
  37.4 1.2 %collective-permute-done.9 = f32[2,64,512]{2,1,0:T(8,128)S(1)} collective-permute-done((f32[2,64,512]{2,1,0:T(8,128)S(1)}, f32[2,64,512]{2,1,0:T(8,128)S(1)}, u32[]{:S(2)}, u32[]{:S(2)}) %collective-permute-start.9) | collective-permute-done | bytes 262176 | tf_op jit(solution)/shard_map/ppermute | solution.py:163
  38.6 0.7 %add.143 = f32[2,64,512]{2,1,0:T(8,128)} add(f32[2,64,512]{2,1,0:T(8,128)S(1)} %get-tuple-element.31, f32[2,64,512]{2,1,0:T(8,128)S(1)} %collective-permute-done.9) | non-fusion elementwise | flops 65536 | bytes 786432 | tf_op jit(solution)/shard_map/add | solution.py:163
  (6 shorter events, 0.1 us)
Async XLA Ops:
  1.8 8.7 %collective-permute-start.1 = (bf16[2,80,512]{2,1,0:T(8,128)(2,1)S(1)}, bf16[2,80,512]{2,1,0:T(8,128)(2,1)S(1)}, u32[]{:S(2)}, u32[]{:S(2)}) collective-permute-start(bf16[2,80,512]{2,1,0:T(8,128)(2,1)S(1)} %maximum_maximum_fusion.packet), channel_id=1, source_target_pairs={{4,0},{8,4},{12,8},{14,12},{10,14},{6,10},{2,6},{0,2},{5,1},{9,5},... | collective-permute-start | bytes 491528 | tf_op jit(solution)/shard_map/ppermute | solution.py:151
  3.9 6.5 %collective-permute-start = (bf16[2,80,512]{2,1,0:T(8,128)(2,1)S(1)}, bf16[2,80,512]{2,1,0:T(8,128)(2,1)S(1)}, u32[]{:S(2)}, u32[]{:S(2)}) collective-permute-start(bf16[2,80,512]{2,1,0:T(8,128)(2,1)S(1)} %maximum_maximum_fusion.packet), channel_id=1, source_target_pairs={{0,4},{4,8},{8,12},{12,14},{14,10},{10,6},{6,2},{2,0},{1,5},{5,9},... | collective-permute-start | bytes 491528 | tf_op jit(solution)/shard_map/ppermute | solution.py:151
  4.0 2.8 %collective-permute-start.2 = (bf16[2,16,512]{2,1,0:T(8,128)(2,1)S(1)}, bf16[2,16,512]{2,1,0:T(8,128)(2,1)S(1)}, u32[]{:S(2)}, u32[]{:S(2)}) collective-permute-start(bf16[2,16,512]{2,1,0:T(8,128)(2,1)S(1)} %concatenate.7), channel_id=1, source_target_pairs={{0,1},{1,0},{2,3},{3,2},{4,5},{5,4},{6,7},{7,6},{8,9},{9,8},{10,11... | collective-permute-start | bytes 98312 | tf_op jit(solution)/shard_map/ppermute | solution.py:95
  10.5 7.4 %collective-permute-start.3 = (bf16[2,80,512]{2,1,0:T(8,128)(2,1)S(1)}, bf16[2,80,512]{2,1,0:T(8,128)(2,1)S(1)}, u32[]{:S(2)}, u32[]{:S(2)}) collective-permute-start(bf16[2,80,512]{2,1,0:T(8,128)(2,1)S(1)} %collective-permute-done.refs_0_), channel_id=1, source_target_pairs={{0,4},{4,8},{8,12},{12,14},{14,10},{10,6},{6,2},{2,0},{1,5},{5,9},... | collective-permute-start | bytes 491528 | tf_op jit(solution)/shard_map/ppermute | solution.py:151
  12.2 5.7 %collective-permute-start.4 = (bf16[2,80,512]{2,1,0:T(8,128)(2,1)S(1)}, bf16[2,80,512]{2,1,0:T(8,128)(2,1)S(1)}, u32[]{:S(2)}, u32[]{:S(2)}) collective-permute-start(bf16[2,80,512]{2,1,0:T(8,128)(2,1)S(1)} %collective-permute-done.1.refs_1_), channel_id=1, source_target_pairs={{4,0},{8,4},{12,8},{14,12},{10,14},{6,10},{2,6},{0,2},{5,1},{9,5},... | collective-permute-start | bytes 491528 | tf_op jit(solution)/shard_map/ppermute | solution.py:151
  17.9 7.2 %collective-permute-start.5 = (bf16[2,80,512]{2,1,0:T(8,128)(2,1)S(1)}, bf16[2,80,512]{2,1,0:T(8,128)(2,1)S(1)}, u32[]{:S(2)}, u32[]{:S(2)}) collective-permute-start(bf16[2,80,512]{2,1,0:T(8,128)(2,1)S(1)} %collective-permute-done.3.refs_0_), channel_id=1, source_target_pairs={{0,4},{4,8},{8,12},{12,14},{14,10},{10,6},{6,2},{2,0},{1,5},{5,9},... | collective-permute-start | bytes 491528 | tf_op jit(solution)/shard_map/ppermute | solution.py:151
  19.4 5.7 %collective-permute-start.6 = (bf16[2,80,512]{2,1,0:T(8,128)(2,1)S(1)}, bf16[2,80,512]{2,1,0:T(8,128)(2,1)S(1)}, u32[]{:S(2)}, u32[]{:S(2)}) collective-permute-start(bf16[2,80,512]{2,1,0:T(8,128)(2,1)S(1)} %collective-permute-done.4.refs_1_), channel_id=1, source_target_pairs={{4,0},{8,4},{12,8},{14,12},{10,14},{6,10},{2,6},{0,2},{5,1},{9,5},... | collective-permute-start | bytes 491528 | tf_op jit(solution)/shard_map/ppermute | solution.py:151
  25.2 7.4 %collective-permute-start.7 = (bf16[1,80,512]{2,1,0:T(8,128)(2,1)S(1)}, bf16[1,80,512]{2,1,0:T(8,128)(2,1)S(1)}, u32[]{:S(2)}, u32[]{:S(2)}) collective-permute-start(bf16[1,80,512]{2,1,0:T(8,128)(2,1)S(1)} %slice.8), channel_id=1, source_target_pairs={{0,4},{4,8},{8,12},{12,14},{14,10},{10,6},{6,2},{2,0},{1,5},{5,9},... | collective-permute-start | bytes 245768 | tf_op jit(solution)/shard_map/ppermute | solution.py:151
  26.7 5.9 %collective-permute-start.8 = (bf16[1,80,512]{2,1,0:T(8,128)(2,1)S(1)}, bf16[1,80,512]{2,1,0:T(8,128)(2,1)S(1)}, u32[]{:S(2)}, u32[]{:S(2)}) collective-permute-start(bf16[1,80,512]{2,1,0:T(8,128)(2,1)S(1)} %slice.9), channel_id=1, source_target_pairs={{4,0},{8,4},{12,8},{14,12},{10,14},{6,10},{2,6},{0,2},{5,1},{9,5},... | collective-permute-start | bytes 245768 | tf_op jit(solution)/shard_map/ppermute | solution.py:151
  35.6 3.0 %collective-permute-start.9 = (f32[2,64,512]{2,1,0:T(8,128)S(1)}, f32[2,64,512]{2,1,0:T(8,128)S(1)}, u32[]{:S(2)}, u32[]{:S(2)}) collective-permute-start(f32[2,64,512]{2,1,0:T(8,128)S(1)} %get-tuple-element.32), channel_id=1, source_target_pairs={{0,1},{1,0},{2,3},{3,2},{4,5},{5,4},{6,7},{7,6},{8,9},{9,8},{10,11... | collective-permute-start | bytes 786440 | tf_op jit(solution)/shard_map/ppermute | solution.py:163

commit v3 on v2

--- a/solution.py
+++ b/solution.py
@@ -1,3 +1,5 @@
+from functools import partial
+
 import jax
 import jax.numpy as jnp
 import numpy as np
@@ -11,7 +13,7 @@
 NN = (((1,), (0,)), ((), ()))
 NT = (((1,), (1,)), ((), ()))
 COLS = 64
-PACK = 80
+PACK = 72
 VM = pl.BlockSpec(memory_space=pltpu.VMEM)
 PARAMS = pltpu.CompilerParams(vmem_limit_bytes=44 * 2**20)
 
@@ -23,23 +25,24 @@
     return [s0, s1, s - s0 - s1]
 
 
-def tiles(sources, weights, offset, left, tangents, acc, d0, d1, k0, k1):
+def tiles(sources, weights, offset, left, tangents, acc, d0, d1, k0, k1, start=0):
     dist, kern = (d0, d1), (k0, k1)
     nc, half = left.shape[0], d0.shape[1]
+    cells = slice(start, start + d0.shape[0])
     for j, source in enumerate(sources):
         nd = source.shape[0]
 
         def one(d, carry, source=source, base=offset + sum(s.shape[0] for s in sources[:j])):
-            along = source[d, COLS:PACK].astype(F32)
+            along = source[d][COLS:PACK].astype(F32)
             one_row = jnp.ones_like(along[0:1])
             rows = jnp.concatenate([along[0:3]] + [one_row] * 3 + squares(along) + [jnp.zeros((7, half), F32)], 0)
             rows = rows.astype(BF16)
             for c in range(nc):
-                dist[c][...] = lax.dot_general(left[c], rows, NN, preferred_element_type=F32)
+                dist[c][...] = lax.dot_general(left[c, cells], rows, NN, preferred_element_type=F32)
             for c in range(nc):
                 coupling = 0.0
                 for k in range(3):
-                    coupling = coupling + jnp.concatenate([tangents[c, k]] * (half // 128), 1) * along[3 + k : 4 + k]
+                    coupling = coupling + jnp.concatenate([tangents[c, k, cells]] * (half // 128), 1) * along[3 + k : 4 + k]
                 kern[c][...] = (coupling * lax.rsqrt(dist[c][...])).astype(BF16)
             for c in range(nc):
                 part = lax.dot_general(kern[c][...], source[d, 0:COLS], NT, preferred_element_type=F32)
@@ -52,7 +55,7 @@
 def first_kernel(packet, other, weights, acc, left, tangents, d0, d1, k0, k1):
     half = other.shape[2]
     for c in range(left.shape[0]):
-        for h, rows in enumerate((packet[c, COLS:PACK], other[c])):
+        for h, rows in enumerate((packet[c][COLS:PACK], other[c])):
             g = rows.astype(F32)
             cells = slice(h * half, (h + 1) * half)
             one_row = jnp.ones_like(g[0:1])
@@ -70,13 +73,12 @@
     tiles((up, down), weights, offset, left, tangents, acc, d0, d1, k0, k1)
 
 
-def last_kernel(offset, up, down, weights, left, tangents, acc_in, keep, send, acc, d0, d1, k0, k1):
-    acc[...] = acc_in[...]
-    tiles((up, down), weights, offset, left, tangents, acc, d0, d1, k0, k1)
-    half = keep.shape[2]
-    for c in range(keep.shape[0]):
-        keep[c] = acc[c, 0:half].T
-        send[c] = acc[c, half:].T
+def last_kernel(offset, start, up, down, weights, left, tangents, acc_in, out, acc, d0, d1, k0, k1):
+    half = out.shape[2]
+    acc[...] = acc_in[:, start : start + half]
+    tiles((up, down), weights, offset, left, tangents, acc, d0, d1, k0, k1, start)
+    for c in range(out.shape[0]):
+        out[c] = acc[c].T
 
 
 def ring_of(n):
@@ -133,13 +135,13 @@
         compiler_params=PARAMS,
         cost_estimate=cost(nc),
     )(packet, other, weights)
-    def call(kernel, outs, extra, offset, up, down, acc, **kw):
+    def call(kernel, outs, scratch, up, down, acc, **kw):
         return pl.pallas_call(
-            lambda *refs: kernel(offset, *refs),
+            kernel,
             out_shape=outs,
             in_specs=[VM] * 6,
-            out_specs=jax.tree.map(lambda _: VM, outs),
-            scratch_shapes=extra + scratch,
+            out_specs=VM,
+            scratch_shapes=scratch,
             compiler_params=PARAMS,
             cost_estimate=cost(up.shape[0] + down.shape[0]),
             **kw,
@@ -155,12 +157,16 @@
     for s in range(1, steps):
         up, down, acc = lax.optimization_barrier((up, down, acc))
         coming = send_on(s + 1, up, down)
-        acc = call(step_kernel, acc_shape, [], offset, up, down, acc, input_output_aliases={5: 0})
+        acc = call(partial(step_kernel, offset), acc_shape, scratch, up, down, acc, input_output_aliases={5: 0})
         offset += 2 * nc
         up, down = coming
     part = shape((nc, COLS, half), F32)
-    keep, send = call(last_kernel, (part, part), [pltpu.VMEM(acc_shape.shape, F32)], offset, up, down, acc)
-    return keep + lax.ppermute(send, "col", [(0, 1), (1, 0)])
+    small = [pltpu.VMEM((nc, half, COLS), F32)]
+    small += [pltpu.VMEM((half, half), F32)] * 2 + [pltpu.VMEM((half, half), BF16)] * 2
+    send = call(partial(last_kernel, offset, half), part, small, up, down, acc)
+    received = lax.ppermute(send, "col", [(0, 1), (1, 0)])
+    keep = call(partial(last_kernel, offset, 0), part, small, up, down, acc)
+    return keep + received
 
 
 def solution(mesh):

time: 39.9 us -> 38.4 us (0.962)
  waiting for transfers between devices: 1.19 us -> 0.03 us
    ppermute x1, waiting for transfers between devices: 1.16 us -> 0.01 us  [body(): received = lax.ppermute(send, 'col', [(0, 1), (1, 0)])]
    pallas_call x4 -> x5, Pallas kernels: 20 us -> 20.3 us  [call(): pl.pallas_call(kernel, out_shape=outs, in_specs=[VM] * 6, out_specs=VM, s...]
  transfers between devices with their start and end apart: 10 -> 10, of which waited for: 1 -> 0; matrix products, arithmetic and copies ran while one was open for 5% -> 5% of each run, Pallas kernels for 52% -> 58%
where the time goes in v3:
time: 38.4 us; the launch traced here: 38.1 us
  Pallas kernels  23.8 us (62%)
  starting transfers between devices  9.67 us (25%)
  other arithmetic  3.57 us (9%)
  local copies, waits for them, and re-layouts  0.88 us (2%)
    pallas_call x5, Pallas kernels, call(): pl.pallas_call(kernel, out_shape=outs, in_specs=[VM] * 6, out_specs=VM, s...  20.3 us
    ppermute x4, starting transfers between devices, send_on(): lax.ppermute(up, 'row', forward)  4.84 us
    pallas_call x1, Pallas kernels, body(): pl.pallas_call(first_kernel, out_shape=(acc_shape, shape((nc, cells, 16),...  3.52 us
    ppermute x4, starting transfers between devices, send_on(): lax.ppermute(down, 'row', backward)  2.37 us
    ppermute x1, starting transfers between devices, body(): received = lax.ppermute(send, 'col', [(0, 1), (1, 0)])  1.51 us
    concatenate x1, other arithmetic, body(): packet = jnp.concatenate([currents, geometry, spare], 1)  0.99 us
    ppermute x1, starting transfers between devices, body(): other = lax.ppermute(packet[:, COLS:PACK], 'col', [(0, 1), (1, 0)])  0.96 us
    reduce_sum x1, other arithmetic, body(): jnp.sum(jnp.where(np.tri(clusters, dtype=bool), pair_count[None, :], 0), 1)  0.8 us
  transfers between devices with their start and end apart: 10, of which 0 were waited for; matrix products, arithmetic and copies ran while one was open for 5% of the time, Pallas kernels for 58%

profile of v3, /device:TPU:1, one launch (start us, length us, event | category | flops | bytes accessed | tf_op | source)
XLA Modules:
  0.0 38.1 jit_solution(1649858225066187948)
XLA Ops:
  0.0 0.7 %copy.11 = bf16[2,7,512]{2,1,0:T(8,128)(2,1)S(1)} copy(bf16[2,7,512]{2,0,1:T(2,128)(2,1)} %param.5) | data formatting | bytes 28672 | tf_op args[0]
  0.7 0.1 pad.3.clone
  0.8 1.0 %maximum_maximum_fusion.packet = bf16[2,72,512]{2,1,0:T(8,128)(2,1)S(1)} fusion(bf16[2,7,512]{2,1,0:T(8,128)(2,1)S(1)} %copy.11, bf16[2,64,512]{2,1,0:T(8,128)(2,1)} %param.6, bf16[72]{0:T(256)(128)(2,1)S(1)} %pad.3.clone), kind=kLoop, calls=%fused_computation | loop fusion | flops 442368 | bytes 293008 | tf_op jit(solution)/shard_map/concatenate | solution.py:96
  1.8 2.1 %collective-permute-start.1 = (bf16[2,72,512]{2,1,0:T(8,128)(2,1)S(1)}, bf16[2,72,512]{2,1,0:T(8,128)(2,1)S(1)}, u32[]{:S(2)}, u32[]{:S(2)}) collective-permute-start(bf16[2,72,512]{2,1,0:T(8,128)(2,1)S(1)} %maximum_maximum_fusion.packet), channel_id=1, source_target_pairs={{4,0},{8,4},{12,8},{14,12},{10,14},{6,10},{2,6},{0,2},{5,1},{9,5},... | collective-permute-start | bytes 442376 | tf_op jit(solution)/shard_map/ppermute | solution.py:153
  3.9 0.1 collective-permute-start
  4.0 1.0 %collective-permute-start.2 = (bf16[2,8,512]{2,1,0:T(8,128)(2,1)S(1)}, bf16[2,8,512]{2,1,0:T(8,128)(2,1)S(1)}, u32[]{:S(2)}, u32[]{:S(2)}) collective-permute-start(bf16[2,8,512]{2,1,0:T(8,128)(2,1)S(1)} %concatenate.7), channel_id=1, source_target_pairs={{0,1},{1,0},{2,3},{3,2},{4,5},{5,4},{6,7},{7,6},{8,9},{9,8},{10,11... | collective-permute-start | bytes 49160 | tf_op jit(solution)/shard_map/ppermute | solution.py:97
  5.0 0.8 %select_reduce_fusion = s32[16]{0:T(128)S(1)} fusion(pred[16,16]{1,0:T(8,128)(4,1)} %constant.99.clone, s32[16]{0:T(128)} %param.7), kind=kLoop, calls=%fused_computation.4 | loop fusion | flops 496 | bytes 384 | tf_op jit(solution)/shard_map/reduce_sum | solution.py:113
  5.8 0.1 convert_reduce_fusion
  5.9 0.1 broadcast_add_fusion
  6.0 0.7 %multiply_add_fusion.1 = (s32[192]{0:T(256)S(1)}, s32[192]{0:T(256)S(1)}) fusion(s32[192]{0:T(256)} %param.8, s32[192]{0:T(256)S(1)} %convert_reduce_fusion), kind=kLoop, calls=%fused_computation.25 | loop fusion | flops 768 | bytes 3072 | tf_op jit(solution)/shard_map/add | solution.py:115
  6.7 0.2 add_reduce_fusion
  6.8 0.0 collective-permute-done.2.other
  6.8 0.1 broadcast_in_dim.19.weights
  6.9 3.5 %shard_map.55 = (f32[2,1024,64]{2,1,0:T(8,128)S(1)}, bf16[2,1024,16]{2,1,0:T(8,128)(2,1)S(1)}, f32[2,3,1024,128]{3,2,1,0:T(8,128)S(1)}) custom-call(bf16[2,72,512]{2,1,0:T(8,128)(2,1)S(1)} %maximum_maximum_fusion.packet, bf16[2,8,512]{2,1,0:T(8,128)(2,1)S(1)} %collective-permute-done.2.other, f32[2,16,64]{2,1,0:T(8,128)S(1)} %broadcast_in_dim.19.weights), custom_call_target="tpu_custom_call" | custom-call | flops 1258291200 | bytes 1048576 | tf_op jit(solution)/shard_map/pallas_call | solution.py:129
  10.4 0.0 collective-permute-done.1.down
  10.5 0.0 collective-permute-done.up
  10.5 1.7 %collective-permute-start.3 = (bf16[2,72,512]{2,1,0:T(8,128)(2,1)S(1)}, bf16[2,72,512]{2,1,0:T(8,128)(2,1)S(1)}, u32[]{:S(2)}, u32[]{:S(2)}) collective-permute-start(bf16[2,72,512]{2,1,0:T(8,128)(2,1)S(1)} %collective-permute-done.up), channel_id=1, source_target_pairs={{0,4},{4,8},{8,12},{12,14},{14,10},{10,6},{6,2},{2,0},{1,5},{5,9},... | collective-permute-start | bytes 442376 | tf_op jit(solution)/shard_map/ppermute | solution.py:153
  12.2 0.0 collective-permute-start.4
  12.2 5.7 %shard_map.56.acc_in = f32[2,1024,64]{2,1,0:T(8,128)S(1)} custom-call(bf16[2,72,512]{2,1,0:T(8,128)(2,1)S(1)} %collective-permute-done.up, bf16[2,72,512]{2,1,0:T(8,128)(2,1)S(1)} %collective-permute-done.1.down, f32[2,16,64]{2,1,0:T(8,128)S(1)} %broadcast_in_dim.19.weights, ...), custom_call_target="tpu_custom_call", output_to_operand_aliasing={{}: (5, {})} | custom-call | flops 2516582400 | bytes 1048576 | tf_op jit(solution)/shard_map/pallas_call | solution.py:139
  17.9 0.0 collective-permute-done.3.up
  17.9 0.0 collective-permute-done.4.down
  17.9 1.5 %collective-permute-start.5 = (bf16[2,72,512]{2,1,0:T(8,128)(2,1)S(1)}, bf16[2,72,512]{2,1,0:T(8,128)(2,1)S(1)}, u32[]{:S(2)}, u32[]{:S(2)}) collective-permute-start(bf16[2,72,512]{2,1,0:T(8,128)(2,1)S(1)} %collective-permute-done.3.up), channel_id=1, source_target_pairs={{0,4},{4,8},{8,12},{12,14},{14,10},{10,6},{6,2},{2,0},{1,5},{5,9},... | collective-permute-start | bytes 442376 | tf_op jit(solution)/shard_map/ppermute | solution.py:153
  19.4 0.0 collective-permute-start.6
  19.4 5.7 %shard_map.57.acc_in = f32[2,1024,64]{2,1,0:T(8,128)S(1)} custom-call(bf16[2,72,512]{2,1,0:T(8,128)(2,1)S(1)} %collective-permute-done.3.up, bf16[2,72,512]{2,1,0:T(8,128)(2,1)S(1)} %collective-permute-done.4.down, f32[2,16,64]{2,1,0:T(8,128)S(1)} %broadcast_in_dim.19.weights, ...), custom_call_target="tpu_custom_call", output_to_operand_aliasing={{}: (5, {})} | custom-call | flops 2516582400 | bytes 1048576 | tf_op jit(solution)/shard_map/pallas_call | solution.py:139
  25.1 0.0 collective-permute-done.5.up
  25.1 0.0 collective-permute-done.6.down
  25.1 1.5 %collective-permute-start.7 = (bf16[1,72,512]{2,1,0:T(8,128)(2,1)S(1)}, bf16[1,72,512]{2,1,0:T(8,128)(2,1)S(1)}, u32[]{:S(2)}, u32[]{:S(2)}) collective-permute-start(bf16[1,72,512]{2,1,0:T(8,128)(2,1)S(1)} %slice.8), channel_id=1, source_target_pairs={{0,4},{4,8},{8,12},{12,14},{14,10},{10,6},{6,2},{2,0},{1,5},{5,9},... | collective-permute-start | bytes 221192 | tf_op jit(solution)/shard_map/ppermute | solution.py:153
  26.6 0.2 collective-permute-start.8
  26.8 5.7 %shard_map.58.acc_in = f32[2,1024,64]{2,1,0:T(8,128)S(1)} custom-call(bf16[2,72,512]{2,1,0:T(8,128)(2,1)S(1)} %collective-permute-done.5.up, bf16[2,72,512]{2,1,0:T(8,128)(2,1)S(1)} %collective-permute-done.6.down, f32[2,16,64]{2,1,0:T(8,128)S(1)} %broadcast_in_dim.19.weights, ...), custom_call_target="tpu_custom_call", output_to_operand_aliasing={{}: (5, {})} | custom-call | flops 2516582400 | bytes 1048576 | tf_op jit(solution)/shard_map/pallas_call | solution.py:139
  32.5 0.0 collective-permute-done.7.up
  32.5 0.0 collective-permute-done.8.down
  32.5 1.6 %shard_map.60 = f32[2,64,512]{2,1,0:T(8,128)S(1)} custom-call(bf16[1,72,512]{2,1,0:T(8,128)(2,1)S(1)} %collective-permute-done.7.up, bf16[1,72,512]{2,1,0:T(8,128)(2,1)S(1)} %collective-permute-done.8.down, f32[2,16,64]{2,1,0:T(8,128)S(1)} %broadcast_in_dim.19.weights, bf16[2,1024,16]{2,1,0:T(8,128)(2,1)S(1)} %get-tuple-element.20.left, ...), custom_call_target="tpu_custom_call" | custom-call | flops 1258291200 | bytes 1048576 | tf_op jit(solution)/shard_map/pallas_call | solution.py:139
  34.2 1.5 %collective-permute-start.9 = (f32[2,64,512]{2,1,0:T(8,128)S(1)}, f32[2,64,512]{2,1,0:T(8,128)S(1)}, u32[]{:S(2)}, u32[]{:S(2)}) collective-permute-start(f32[2,64,512]{2,1,0:T(8,128)S(1)} %shard_map.60), channel_id=1, source_target_pairs={{0,1},{1,0},{2,3},{3,2},{4,5},{5,4},{6,7},{7,6},{8,9},{9,8},{10,11... | collective-permute-start | bytes 786440 | tf_op jit(solution)/shard_map/ppermute | solution.py:167
  35.7 1.6 %shard_map.59 = f32[2,64,512]{2,1,0:T(8,128)S(1)} custom-call(bf16[1,72,512]{2,1,0:T(8,128)(2,1)S(1)} %collective-permute-done.7.up, bf16[1,72,512]{2,1,0:T(8,128)(2,1)S(1)} %collective-permute-done.8.down, f32[2,16,64]{2,1,0:T(8,128)S(1)} %broadcast_in_dim.19.weights, bf16[2,1024,16]{2,1,0:T(8,128)(2,1)S(1)} %get-tuple-element.20.left, ...), custom_call_target="tpu_custom_call" | custom-call | flops 1258291200 | bytes 1048576 | tf_op jit(solution)/shard_map/pallas_call | solution.py:139
  37.3 0.0 collective-permute-done.9
  37.3 0.7 %add.143 = f32[2,64,512]{2,1,0:T(8,128)} add(f32[2,64,512]{2,1,0:T(8,128)S(1)} %shard_map.59, f32[2,64,512]{2,1,0:T(8,128)S(1)} %collective-permute-done.9) | non-fusion elementwise | flops 65536 | bytes 786432 | tf_op jit(solution)/shard_map/add | solution.py:169
  (5 shorter events, 0.0 us)
Async XLA Ops:
  1.8 8.7 %collective-permute-start.1 = (bf16[2,72,512]{2,1,0:T(8,128)(2,1)S(1)}, bf16[2,72,512]{2,1,0:T(8,128)(2,1)S(1)}, u32[]{:S(2)}, u32[]{:S(2)}) collective-permute-start(bf16[2,72,512]{2,1,0:T(8,128)(2,1)S(1)} %maximum_maximum_fusion.packet), channel_id=1, source_target_pairs={{4,0},{8,4},{12,8},{14,12},{10,14},{6,10},{2,6},{0,2},{5,1},{9,5},... | collective-permute-start | bytes 442376 | tf_op jit(solution)/shard_map/ppermute | solution.py:153
  3.9 6.5 %collective-permute-start = (bf16[2,72,512]{2,1,0:T(8,128)(2,1)S(1)}, bf16[2,72,512]{2,1,0:T(8,128)(2,1)S(1)}, u32[]{:S(2)}, u32[]{:S(2)}) collective-permute-start(bf16[2,72,512]{2,1,0:T(8,128)(2,1)S(1)} %maximum_maximum_fusion.packet), channel_id=1, source_target_pairs={{0,4},{4,8},{8,12},{12,14},{14,10},{10,6},{6,2},{2,0},{1,5},{5,9},... | collective-permute-start | bytes 442376 | tf_op jit(solution)/shard_map/ppermute | solution.py:153
  4.0 2.8 %collective-permute-start.2 = (bf16[2,8,512]{2,1,0:T(8,128)(2,1)S(1)}, bf16[2,8,512]{2,1,0:T(8,128)(2,1)S(1)}, u32[]{:S(2)}, u32[]{:S(2)}) collective-permute-start(bf16[2,8,512]{2,1,0:T(8,128)(2,1)S(1)} %concatenate.7), channel_id=1, source_target_pairs={{0,1},{1,0},{2,3},{3,2},{4,5},{5,4},{6,7},{7,6},{8,9},{9,8},{10,11... | collective-permute-start | bytes 49160 | tf_op jit(solution)/shard_map/ppermute | solution.py:97
  10.5 7.4 %collective-permute-start.3 = (bf16[2,72,512]{2,1,0:T(8,128)(2,1)S(1)}, bf16[2,72,512]{2,1,0:T(8,128)(2,1)S(1)}, u32[]{:S(2)}, u32[]{:S(2)}) collective-permute-start(bf16[2,72,512]{2,1,0:T(8,128)(2,1)S(1)} %collective-permute-done.up), channel_id=1, source_target_pairs={{0,4},{4,8},{8,12},{12,14},{14,10},{10,6},{6,2},{2,0},{1,5},{5,9},... | collective-permute-start | bytes 442376 | tf_op jit(solution)/shard_map/ppermute | solution.py:153
  12.2 5.7 %collective-permute-start.4 = (bf16[2,72,512]{2,1,0:T(8,128)(2,1)S(1)}, bf16[2,72,512]{2,1,0:T(8,128)(2,1)S(1)}, u32[]{:S(2)}, u32[]{:S(2)}) collective-permute-start(bf16[2,72,512]{2,1,0:T(8,128)(2,1)S(1)} %collective-permute-done.1.down), channel_id=1, source_target_pairs={{4,0},{8,4},{12,8},{14,12},{10,14},{6,10},{2,6},{0,2},{5,1},{9,5},... | collective-permute-start | bytes 442376 | tf_op jit(solution)/shard_map/ppermute | solution.py:153
  17.9 7.2 %collective-permute-start.5 = (bf16[2,72,512]{2,1,0:T(8,128)(2,1)S(1)}, bf16[2,72,512]{2,1,0:T(8,128)(2,1)S(1)}, u32[]{:S(2)}, u32[]{:S(2)}) collective-permute-start(bf16[2,72,512]{2,1,0:T(8,128)(2,1)S(1)} %collective-permute-done.3.up), channel_id=1, source_target_pairs={{0,4},{4,8},{8,12},{12,14},{14,10},{10,6},{6,2},{2,0},{1,5},{5,9},... | collective-permute-start | bytes 442376 | tf_op jit(solution)/shard_map/ppermute | solution.py:153
  19.4 5.7 %collective-permute-start.6 = (bf16[2,72,512]{2,1,0:T(8,128)(2,1)S(1)}, bf16[2,72,512]{2,1,0:T(8,128)(2,1)S(1)}, u32[]{:S(2)}, u32[]{:S(2)}) collective-permute-start(bf16[2,72,512]{2,1,0:T(8,128)(2,1)S(1)} %collective-permute-done.4.down), channel_id=1, source_target_pairs={{4,0},{8,4},{12,8},{14,12},{10,14},{6,10},{2,6},{0,2},{5,1},{9,5},... | collective-permute-start | bytes 442376 | tf_op jit(solution)/shard_map/ppermute | solution.py:153
  25.1 7.4 %collective-permute-start.7 = (bf16[1,72,512]{2,1,0:T(8,128)(2,1)S(1)}, bf16[1,72,512]{2,1,0:T(8,128)(2,1)S(1)}, u32[]{:S(2)}, u32[]{:S(2)}) collective-permute-start(bf16[1,72,512]{2,1,0:T(8,128)(2,1)S(1)} %slice.8), channel_id=1, source_target_pairs={{0,4},{4,8},{8,12},{12,14},{14,10},{10,6},{6,2},{2,0},{1,5},{5,9},... | collective-permute-start | bytes 221192 | tf_op jit(solution)/shard_map/ppermute | solution.py:153
  26.6 5.9 %collective-permute-start.8 = (bf16[1,72,512]{2,1,0:T(8,128)(2,1)S(1)}, bf16[1,72,512]{2,1,0:T(8,128)(2,1)S(1)}, u32[]{:S(2)}, u32[]{:S(2)}) collective-permute-start(bf16[1,72,512]{2,1,0:T(8,128)(2,1)S(1)} %slice.9), channel_id=1, source_target_pairs={{4,0},{8,4},{12,8},{14,12},{10,14},{6,10},{2,6},{0,2},{5,1},{9,5},... | collective-permute-start | bytes 221192 | tf_op jit(solution)/shard_map/ppermute | solution.py:153
  34.2 3.2 %collective-permute-start.9 = (f32[2,64,512]{2,1,0:T(8,128)S(1)}, f32[2,64,512]{2,1,0:T(8,128)S(1)}, u32[]{:S(2)}, u32[]{:S(2)}) collective-permute-start(f32[2,64,512]{2,1,0:T(8,128)S(1)} %shard_map.60), channel_id=1, source_target_pairs={{0,1},{1,0},{2,3},{3,2},{4,5},{5,4},{6,7},{7,6},{8,9},{9,8},{10,11... | collective-permute-start | bytes 786440 | tf_op jit(solution)/shard_map/ppermute | solution.py:167

commit v4 on v3

--- a/solution.py
+++ b/solution.py
@@ -2,7 +2,6 @@
 
 import jax
 import jax.numpy as jnp
-import numpy as np
 from jax import lax
 from jax.experimental import pallas as pl
 from jax.experimental.pallas import tpu as pltpu
@@ -110,7 +109,10 @@
     else:
         chip = (row + shift + n) % n
     second = chip * nc + jnp.arange(n * nc) % nc
-    ends = jnp.sum(jnp.where(np.tri(clusters, dtype=bool), pair_count[None, :], 0), 1)
+    lists = lax.optimization_barrier(jnp.concatenate([pair_count, pair_target]))
+    pair_count, pair_target = lists[:clusters], lists[clusters:]
+    upto = jnp.arange(clusters)[:, None] >= jnp.arange(clusters)[None, :]
+    ends = jnp.sum(jnp.where(upto, pair_count[None, :], 0), 1)
     first_of = jnp.sum((ends[:, None] <= jnp.arange(pair_target.shape[0])[None, :]).astype(jnp.int32), 0)
     listed = first_of * clusters + pair_target
     turned = pair_target * clusters + first_of

time: 38.4 us -> 37.8 us (0.984)
  other arithmetic: 3.57 us -> 3.03 us
    concatenate x0 -> x1, other arithmetic: none -> 0.76 us  [body(): lists = lax.optimization_barrier(jnp.concatenate([pair_count, pair_target]))]
    reduce_sum x1, other arithmetic: 0.8 us -> 0.12 us  [body(): ends = jnp.sum(jnp.where(upto, pair_count[None, :], 0), 1)]
    add x1, other arithmetic: 0.68 us -> 0.07 us  [body(): listed = first_of * clusters + pair_target]
  transfers between devices with their start and end apart: 10 -> 10, of which waited for: 0 -> 0; matrix products, arithmetic and copies ran while one was open for 5% -> 4% of each run, Pallas kernels for 58% -> 59%
where the time goes in v4:
time: 37.8 us; the launch traced here: 37.6 us
  Pallas kernels  23.8 us (63%)
  starting transfers between devices  9.68 us (26%)
  other arithmetic  3.03 us (8%)
  local copies, waits for them, and re-layouts  0.88 us (2%)
    pallas_call x5, Pallas kernels, call(): pl.pallas_call(kernel, out_shape=outs, in_specs=[VM] * 6, out_specs=VM, s...  20.3 us
    ppermute x4, starting transfers between devices, send_on(): lax.ppermute(up, 'row', forward)  4.88 us
    pallas_call x1, Pallas kernels, body(): pl.pallas_call(first_kernel, out_shape=(acc_shape, shape((nc, cells, 16),...  3.52 us
    ppermute x4, starting transfers between devices, send_on(): lax.ppermute(down, 'row', backward)  2.33 us
    ppermute x1, starting transfers between devices, body(): received = lax.ppermute(send, 'col', [(0, 1), (1, 0)])  1.52 us
    concatenate x1, other arithmetic, body(): packet = jnp.concatenate([currents, geometry, spare], 1)  0.99 us
    ppermute x1, starting transfers between devices, body(): other = lax.ppermute(packet[:, COLS:PACK], 'col', [(0, 1), (1, 0)])  0.96 us
    concatenate x1, other arithmetic, body(): lists = lax.optimization_barrier(jnp.concatenate([pair_count, pair_target]))  0.76 us
  transfers between devices with their start and end apart: 10, of which 0 were waited for; matrix products, arithmetic and copies ran while one was open for 4% of the time, Pallas kernels for 59%

profile of v4, /device:TPU:1, one launch (start us, length us, event | category | flops | bytes accessed | tf_op | source)
XLA Modules:
  0.0 37.6 jit_solution(17817507936380269657)
XLA Ops:
  0.0 0.7 %copy.10 = bf16[2,7,512]{2,1,0:T(8,128)(2,1)S(1)} copy(bf16[2,7,512]{2,0,1:T(2,128)(2,1)} %param.4) | data formatting | bytes 28672 | tf_op args[0]
  0.7 0.1 pad.5.clone
  0.8 1.0 %maximum_maximum_fusion.packet = bf16[2,72,512]{2,1,0:T(8,128)(2,1)S(1)} fusion(bf16[2,7,512]{2,1,0:T(8,128)(2,1)S(1)} %copy.10, bf16[2,64,512]{2,1,0:T(8,128)(2,1)} %param.5, bf16[72]{0:T(256)(128)(2,1)S(1)} %pad.5.clone), kind=kLoop, calls=%fused_computation | loop fusion | flops 442368 | bytes 293008 | tf_op jit(solution)/shard_map/concatenate | solution.py:95
  1.8 2.1 %collective-permute-start.1 = (bf16[2,72,512]{2,1,0:T(8,128)(2,1)S(1)}, bf16[2,72,512]{2,1,0:T(8,128)(2,1)S(1)}, u32[]{:S(2)}, u32[]{:S(2)}) collective-permute-start(bf16[2,72,512]{2,1,0:T(8,128)(2,1)S(1)} %maximum_maximum_fusion.packet), channel_id=1, source_target_pairs={{4,0},{8,4},{12,8},{14,12},{10,14},{6,10},{2,6},{0,2},{5,1},{9,5},... | collective-permute-start | bytes 442376 | tf_op jit(solution)/shard_map/ppermute | solution.py:155
  3.9 0.1 collective-permute-start
  4.0 1.0 %collective-permute-start.2 = (bf16[2,8,512]{2,1,0:T(8,128)(2,1)S(1)}, bf16[2,8,512]{2,1,0:T(8,128)(2,1)S(1)}, u32[]{:S(2)}, u32[]{:S(2)}) collective-permute-start(bf16[2,8,512]{2,1,0:T(8,128)(2,1)S(1)} %concatenate.10), channel_id=1, source_target_pairs={{0,1},{1,0},{2,3},{3,2},{4,5},{5,4},{6,7},{7,6},{8,9},{9,8},{10,11... | collective-permute-start | bytes 49160 | tf_op jit(solution)/shard_map/ppermute | solution.py:96
  5.0 0.8 %pad_add_fusion = s32[208]{0:T(256)S(1)} fusion(s32[192]{0:T(256)} %param.7, s32[16]{0:T(128)} %param.6), kind=kLoop, calls=%fused_computation.22 | loop fusion | flops 208 | bytes 1664 | tf_op jit(solution)/shard_map/concatenate | solution.py:112
  5.8 0.1 select_reduce_fusion
  5.9 0.1 convert_reduce_fusion
  6.0 0.1 multiply_add_fusion.1
  6.1 0.1 broadcast_add_fusion
  6.2 0.2 add_reduce_fusion
  6.3 0.0 collective-permute-done.2.other
  6.3 0.1 broadcast_in_dim.19.weights
  6.4 3.5 %shard_map.46 = (f32[2,1024,64]{2,1,0:T(8,128)S(1)}, bf16[2,1024,16]{2,1,0:T(8,128)(2,1)S(1)}, f32[2,3,1024,128]{3,2,1,0:T(8,128)S(1)}) custom-call(bf16[2,72,512]{2,1,0:T(8,128)(2,1)S(1)} %maximum_maximum_fusion.packet, bf16[2,8,512]{2,1,0:T(8,128)(2,1)S(1)} %collective-permute-done.2.other, f32[2,16,64]{2,1,0:T(8,128)S(1)} %broadcast_in_dim.19.weights), custom_call_target="tpu_custom_call" | custom-call | flops 1258291200 | bytes 1048576 | tf_op jit(solution)/shard_map/pallas_call | solution.py:131
  9.9 0.0 collective-permute-done.1.down
  9.9 0.0 collective-permute-done.up
  9.9 1.7 %collective-permute-start.3 = (bf16[2,72,512]{2,1,0:T(8,128)(2,1)S(1)}, bf16[2,72,512]{2,1,0:T(8,128)(2,1)S(1)}, u32[]{:S(2)}, u32[]{:S(2)}) collective-permute-start(bf16[2,72,512]{2,1,0:T(8,128)(2,1)S(1)} %collective-permute-done.up), channel_id=1, source_target_pairs={{0,4},{4,8},{8,12},{12,14},{14,10},{10,6},{6,2},{2,0},{1,5},{5,9},... | collective-permute-start | bytes 442376 | tf_op jit(solution)/shard_map/ppermute | solution.py:155
  11.7 0.0 collective-permute-start.4
  11.7 5.7 %shard_map.47.acc_in = f32[2,1024,64]{2,1,0:T(8,128)S(1)} custom-call(bf16[2,72,512]{2,1,0:T(8,128)(2,1)S(1)} %collective-permute-done.up, bf16[2,72,512]{2,1,0:T(8,128)(2,1)S(1)} %collective-permute-done.1.down, f32[2,16,64]{2,1,0:T(8,128)S(1)} %broadcast_in_dim.19.weights, ...), custom_call_target="tpu_custom_call", output_to_operand_aliasing={{}: (5, {})} | custom-call | flops 2516582400 | bytes 1048576 | tf_op jit(solution)/shard_map/pallas_call | solution.py:141
  17.4 0.0 collective-permute-done.3.up
  17.4 0.0 collective-permute-done.4.down
  17.4 1.5 %collective-permute-start.5 = (bf16[2,72,512]{2,1,0:T(8,128)(2,1)S(1)}, bf16[2,72,512]{2,1,0:T(8,128)(2,1)S(1)}, u32[]{:S(2)}, u32[]{:S(2)}) collective-permute-start(bf16[2,72,512]{2,1,0:T(8,128)(2,1)S(1)} %collective-permute-done.3.up), channel_id=1, source_target_pairs={{0,4},{4,8},{8,12},{12,14},{14,10},{10,6},{6,2},{2,0},{1,5},{5,9},... | collective-permute-start | bytes 442376 | tf_op jit(solution)/shard_map/ppermute | solution.py:155
  18.9 0.0 collective-permute-start.6
  18.9 5.7 %shard_map.48.acc_in = f32[2,1024,64]{2,1,0:T(8,128)S(1)} custom-call(bf16[2,72,512]{2,1,0:T(8,128)(2,1)S(1)} %collective-permute-done.3.up, bf16[2,72,512]{2,1,0:T(8,128)(2,1)S(1)} %collective-permute-done.4.down, f32[2,16,64]{2,1,0:T(8,128)S(1)} %broadcast_in_dim.19.weights, ...), custom_call_target="tpu_custom_call", output_to_operand_aliasing={{}: (5, {})} | custom-call | flops 2516582400 | bytes 1048576 | tf_op jit(solution)/shard_map/pallas_call | solution.py:141
  24.6 0.0 collective-permute-done.5.up
  24.6 0.0 collective-permute-done.6.down
  24.6 1.5 %collective-permute-start.7 = (bf16[1,72,512]{2,1,0:T(8,128)(2,1)S(1)}, bf16[1,72,512]{2,1,0:T(8,128)(2,1)S(1)}, u32[]{:S(2)}, u32[]{:S(2)}) collective-permute-start(bf16[1,72,512]{2,1,0:T(8,128)(2,1)S(1)} %slice.16), channel_id=1, source_target_pairs={{0,4},{4,8},{8,12},{12,14},{14,10},{10,6},{6,2},{2,0},{1,5},{5,9},... | collective-permute-start | bytes 221192 | tf_op jit(solution)/shard_map/ppermute | solution.py:155
  26.1 0.2 collective-permute-start.8
  26.3 5.7 %shard_map.49.acc_in = f32[2,1024,64]{2,1,0:T(8,128)S(1)} custom-call(bf16[2,72,512]{2,1,0:T(8,128)(2,1)S(1)} %collective-permute-done.5.up, bf16[2,72,512]{2,1,0:T(8,128)(2,1)S(1)} %collective-permute-done.6.down, f32[2,16,64]{2,1,0:T(8,128)S(1)} %broadcast_in_dim.19.weights, ...), custom_call_target="tpu_custom_call", output_to_operand_aliasing={{}: (5, {})} | custom-call | flops 2516582400 | bytes 1048576 | tf_op jit(solution)/shard_map/pallas_call | solution.py:141
  32.0 0.0 collective-permute-done.7.up
  32.0 0.0 collective-permute-done.8.down
  32.0 1.6 %shard_map.51 = f32[2,64,512]{2,1,0:T(8,128)S(1)} custom-call(bf16[1,72,512]{2,1,0:T(8,128)(2,1)S(1)} %collective-permute-done.7.up, bf16[1,72,512]{2,1,0:T(8,128)(2,1)S(1)} %collective-permute-done.8.down, f32[2,16,64]{2,1,0:T(8,128)S(1)} %broadcast_in_dim.19.weights, bf16[2,1024,16]{2,1,0:T(8,128)(2,1)S(1)} %get-tuple-element.20.left, ...), custom_call_target="tpu_custom_call" | custom-call | flops 1258291200 | bytes 1048576 | tf_op jit(solution)/shard_map/pallas_call | solution.py:141
  33.6 1.5 %collective-permute-start.9 = (f32[2,64,512]{2,1,0:T(8,128)S(1)}, f32[2,64,512]{2,1,0:T(8,128)S(1)}, u32[]{:S(2)}, u32[]{:S(2)}) collective-permute-start(f32[2,64,512]{2,1,0:T(8,128)S(1)} %shard_map.51), channel_id=1, source_target_pairs={{0,1},{1,0},{2,3},{3,2},{4,5},{5,4},{6,7},{7,6},{8,9},{9,8},{10,11... | collective-permute-start | bytes 786440 | tf_op jit(solution)/shard_map/ppermute | solution.py:169
  35.2 1.6 %shard_map.50 = f32[2,64,512]{2,1,0:T(8,128)S(1)} custom-call(bf16[1,72,512]{2,1,0:T(8,128)(2,1)S(1)} %collective-permute-done.7.up, bf16[1,72,512]{2,1,0:T(8,128)(2,1)S(1)} %collective-permute-done.8.down, f32[2,16,64]{2,1,0:T(8,128)S(1)} %broadcast_in_dim.19.weights, bf16[2,1024,16]{2,1,0:T(8,128)(2,1)S(1)} %get-tuple-element.20.left, ...), custom_call_target="tpu_custom_call" | custom-call | flops 1258291200 | bytes 1048576 | tf_op jit(solution)/shard_map/pallas_call | solution.py:141
  36.8 0.0 collective-permute-done.9
  36.8 0.7 %add.143 = f32[2,64,512]{2,1,0:T(8,128)} add(f32[2,64,512]{2,1,0:T(8,128)S(1)} %shard_map.50, f32[2,64,512]{2,1,0:T(8,128)S(1)} %collective-permute-done.9) | non-fusion elementwise | flops 65536 | bytes 786432 | tf_op jit(solution)/shard_map/add | solution.py:171
  (6 shorter events, 0.1 us)
Async XLA Ops:
  1.8 8.1 %collective-permute-start.1 = (bf16[2,72,512]{2,1,0:T(8,128)(2,1)S(1)}, bf16[2,72,512]{2,1,0:T(8,128)(2,1)S(1)}, u32[]{:S(2)}, u32[]{:S(2)}) collective-permute-start(bf16[2,72,512]{2,1,0:T(8,128)(2,1)S(1)} %maximum_maximum_fusion.packet), channel_id=1, source_target_pairs={{4,0},{8,4},{12,8},{14,12},{10,14},{6,10},{2,6},{0,2},{5,1},{9,5},... | collective-permute-start | bytes 442376 | tf_op jit(solution)/shard_map/ppermute | solution.py:155
  3.9 6.0 %collective-permute-start = (bf16[2,72,512]{2,1,0:T(8,128)(2,1)S(1)}, bf16[2,72,512]{2,1,0:T(8,128)(2,1)S(1)}, u32[]{:S(2)}, u32[]{:S(2)}) collective-permute-start(bf16[2,72,512]{2,1,0:T(8,128)(2,1)S(1)} %maximum_maximum_fusion.packet), channel_id=1, source_target_pairs={{0,4},{4,8},{8,12},{12,14},{14,10},{10,6},{6,2},{2,0},{1,5},{5,9},... | collective-permute-start | bytes 442376 | tf_op jit(solution)/shard_map/ppermute | solution.py:155
  4.0 2.3 %collective-permute-start.2 = (bf16[2,8,512]{2,1,0:T(8,128)(2,1)S(1)}, bf16[2,8,512]{2,1,0:T(8,128)(2,1)S(1)}, u32[]{:S(2)}, u32[]{:S(2)}) collective-permute-start(bf16[2,8,512]{2,1,0:T(8,128)(2,1)S(1)} %concatenate.10), channel_id=1, source_target_pairs={{0,1},{1,0},{2,3},{3,2},{4,5},{5,4},{6,7},{7,6},{8,9},{9,8},{10,11... | collective-permute-start | bytes 49160 | tf_op jit(solution)/shard_map/ppermute | solution.py:96
  9.9 7.4 %collective-permute-start.3 = (bf16[2,72,512]{2,1,0:T(8,128)(2,1)S(1)}, bf16[2,72,512]{2,1,0:T(8,128)(2,1)S(1)}, u32[]{:S(2)}, u32[]{:S(2)}) collective-permute-start(bf16[2,72,512]{2,1,0:T(8,128)(2,1)S(1)} %collective-permute-done.up), channel_id=1, source_target_pairs={{0,4},{4,8},{8,12},{12,14},{14,10},{10,6},{6,2},{2,0},{1,5},{5,9},... | collective-permute-start | bytes 442376 | tf_op jit(solution)/shard_map/ppermute | solution.py:155
  11.7 5.7 %collective-permute-start.4 = (bf16[2,72,512]{2,1,0:T(8,128)(2,1)S(1)}, bf16[2,72,512]{2,1,0:T(8,128)(2,1)S(1)}, u32[]{:S(2)}, u32[]{:S(2)}) collective-permute-start(bf16[2,72,512]{2,1,0:T(8,128)(2,1)S(1)} %collective-permute-done.1.down), channel_id=1, source_target_pairs={{4,0},{8,4},{12,8},{14,12},{10,14},{6,10},{2,6},{0,2},{5,1},{9,5},... | collective-permute-start | bytes 442376 | tf_op jit(solution)/shard_map/ppermute | solution.py:155
  17.4 7.2 %collective-permute-start.5 = (bf16[2,72,512]{2,1,0:T(8,128)(2,1)S(1)}, bf16[2,72,512]{2,1,0:T(8,128)(2,1)S(1)}, u32[]{:S(2)}, u32[]{:S(2)}) collective-permute-start(bf16[2,72,512]{2,1,0:T(8,128)(2,1)S(1)} %collective-permute-done.3.up), channel_id=1, source_target_pairs={{0,4},{4,8},{8,12},{12,14},{14,10},{10,6},{6,2},{2,0},{1,5},{5,9},... | collective-permute-start | bytes 442376 | tf_op jit(solution)/shard_map/ppermute | solution.py:155
  18.9 5.7 %collective-permute-start.6 = (bf16[2,72,512]{2,1,0:T(8,128)(2,1)S(1)}, bf16[2,72,512]{2,1,0:T(8,128)(2,1)S(1)}, u32[]{:S(2)}, u32[]{:S(2)}) collective-permute-start(bf16[2,72,512]{2,1,0:T(8,128)(2,1)S(1)} %collective-permute-done.4.down), channel_id=1, source_target_pairs={{4,0},{8,4},{12,8},{14,12},{10,14},{6,10},{2,6},{0,2},{5,1},{9,5},... | collective-permute-start | bytes 442376 | tf_op jit(solution)/shard_map/ppermute | solution.py:155
  24.6 7.4 %collective-permute-start.7 = (bf16[1,72,512]{2,1,0:T(8,128)(2,1)S(1)}, bf16[1,72,512]{2,1,0:T(8,128)(2,1)S(1)}, u32[]{:S(2)}, u32[]{:S(2)}) collective-permute-start(bf16[1,72,512]{2,1,0:T(8,128)(2,1)S(1)} %slice.16), channel_id=1, source_target_pairs={{0,4},{4,8},{8,12},{12,14},{14,10},{10,6},{6,2},{2,0},{1,5},{5,9},... | collective-permute-start | bytes 221192 | tf_op jit(solution)/shard_map/ppermute | solution.py:155
  26.1 5.9 %collective-permute-start.8 = (bf16[1,72,512]{2,1,0:T(8,128)(2,1)S(1)}, bf16[1,72,512]{2,1,0:T(8,128)(2,1)S(1)}, u32[]{:S(2)}, u32[]{:S(2)}) collective-permute-start(bf16[1,72,512]{2,1,0:T(8,128)(2,1)S(1)} %slice.17), channel_id=1, source_target_pairs={{4,0},{8,4},{12,8},{14,12},{10,14},{6,10},{2,6},{0,2},{5,1},{9,5},... | collective-permute-start | bytes 221192 | tf_op jit(solution)/shard_map/ppermute | solution.py:155
  33.6 3.2 %collective-permute-start.9 = (f32[2,64,512]{2,1,0:T(8,128)S(1)}, f32[2,64,512]{2,1,0:T(8,128)S(1)}, u32[]{:S(2)}, u32[]{:S(2)}) collective-permute-start(f32[2,64,512]{2,1,0:T(8,128)S(1)} %shard_map.51), channel_id=1, source_target_pairs={{0,1},{1,0},{2,3},{3,2},{4,5},{5,4},{6,7},{7,6},{8,9},{9,8},{10,11... | collective-permute-start | bytes 786440 | tf_op jit(solution)/shard_map/ppermute | solution.py:169

commit v5 on v4

--- a/solution.py
+++ b/solution.py
@@ -24,31 +24,36 @@
     return [s0, s1, s - s0 - s1]
 
 
-def tiles(sources, weights, offset, left, tangents, acc, d0, d1, k0, k1, start=0):
+def tiles(sources, weights, offset, left, tangents, acc, stage, d0, d1, k0, k1, start=0):
     dist, kern = (d0, d1), (k0, k1)
     nc, half = left.shape[0], d0.shape[1]
     cells = slice(start, start + d0.shape[0])
-    for j, source in enumerate(sources):
-        nd = source.shape[0]
+    if stage is not None:
+        whole = [(source, i) for source in sources for i in range(source.shape[0])]
+        for at, (source, i) in enumerate(whole):
+            stage[at] = source[i]
+        sources = (stage,)
 
-        def one(d, carry, source=source, base=offset + sum(s.shape[0] for s in sources[:j])):
-            along = source[d][COLS:PACK].astype(F32)
-            one_row = jnp.ones_like(along[0:1])
-            rows = jnp.concatenate([along[0:3]] + [one_row] * 3 + squares(along) + [jnp.zeros((7, half), F32)], 0)
-            rows = rows.astype(BF16)
-            for c in range(nc):
-                dist[c][...] = lax.dot_general(left[c, cells], rows, NN, preferred_element_type=F32)
-            for c in range(nc):
-                coupling = 0.0
-                for k in range(3):
-                    coupling = coupling + jnp.concatenate([tangents[c, k, cells]] * (half // 128), 1) * along[3 + k : 4 + k]
-                kern[c][...] = (coupling * lax.rsqrt(dist[c][...])).astype(BF16)
-            for c in range(nc):
-                part = lax.dot_general(kern[c][...], source[d, 0:COLS], NT, preferred_element_type=F32)
-                acc[c] += weights[c, pl.ds(base + d, 1)] * part
-            return carry
+    def one(d, carry, source, base):
+        along = source[d][COLS:PACK].astype(F32)
+        one_row = jnp.ones_like(along[0:1])
+        rows = jnp.concatenate([along[0:3]] + [one_row] * 3 + squares(along) + [jnp.zeros((7, half), F32)], 0)
+        rows = rows.astype(BF16)
+        for c in range(nc):
+            dist[c][...] = lax.dot_general(left[c, cells], rows, NN, preferred_element_type=F32)
+        for c in range(nc):
+            coupling = 0.0
+            for k in range(3):
+                coupling = coupling + jnp.concatenate([tangents[c, k, cells]] * (half // 128), 1) * along[3 + k : 4 + k]
+            kern[c][...] = (coupling * lax.rsqrt(dist[c][...])).astype(BF16)
+        for c in range(nc):
+            part = lax.dot_general(kern[c][...], source[d, 0:COLS], NT, preferred_element_type=F32)
+            acc[c] += weights[c, pl.ds(base + d, 1)] * part
+        return carry
 
-        lax.fori_loop(0, nd, one, 0)
+    for source in sources:
+        lax.fori_loop(0, source.shape[0], partial(one, source=source, base=offset), 0)
+        offset += source.shape[0]
 
 
 def first_kernel(packet, other, weights, acc, left, tangents, d0, d1, k0, k1):
@@ -64,18 +69,18 @@
             for k in range(3):
                 tangents[c, k, cells] = jnp.broadcast_to(across[:, k : k + 1], (half, 128))
     acc[...] = jnp.zeros_like(acc)
-    tiles((packet,), weights, 0, left, tangents, acc, d0, d1, k0, k1)
+    tiles((packet,), weights, 0, left, tangents, acc, None, d0, d1, k0, k1)
 
 
-def step_kernel(offset, up, down, weights, left, tangents, acc_in, acc, d0, d1, k0, k1):
+def step_kernel(offset, up, down, weights, left, tangents, acc_in, acc, stage, d0, d1, k0, k1):
     acc[...] = acc_in[...]
-    tiles((up, down), weights, offset, left, tangents, acc, d0, d1, k0, k1)
+    tiles((up, down), weights, offset, left, tangents, acc, stage, d0, d1, k0, k1)
 
 
 def last_kernel(offset, start, up, down, weights, left, tangents, acc_in, out, acc, d0, d1, k0, k1):
     half = out.shape[2]
     acc[...] = acc_in[:, start : start + half]
-    tiles((up, down), weights, offset, left, tangents, acc, d0, d1, k0, k1, start)
+    tiles((up, down), weights, offset, left, tangents, acc, None, d0, d1, k0, k1, start)
     for c in range(out.shape[0]):
         out[c] = acc[c].T
 
@@ -159,7 +164,7 @@
     for s in range(1, steps):
         up, down, acc = lax.optimization_barrier((up, down, acc))
         coming = send_on(s + 1, up, down)
-        acc = call(partial(step_kernel, offset), acc_shape, scratch, up, down, acc, input_output_aliases={5: 0})
+        acc = call(partial(step_kernel, offset), acc_shape, [pltpu.VMEM((2 * nc, PACK, half), BF16)] + scratch, up, down, acc, input_output_aliases={5: 0})
         offset += 2 * nc
         up, down = coming
     part = shape((nc, COLS, half), F32)

time: 37.8 us -> 37.4 us (0.989)
  Pallas kernels: 23.8 us -> 23.2 us
    pallas_call x5, Pallas kernels: 20.3 us -> 19.7 us  [call(): pl.pallas_call(kernel, out_shape=outs, in_specs=[VM] * 6, out_specs=VM, s...]
    ppermute x1, starting transfers between devices: 1.52 us -> 1.9 us  [body(): received = lax.ppermute(send, 'col', [(0, 1), (1, 0)])]
  transfers between devices with their start and end apart: 10 -> 10, of which waited for: 0 -> 0; matrix products, arithmetic and copies ran while one was open for 4% -> 4% of each run, Pallas kernels for 59% -> 58%
where the time goes in v5:
time: 37.4 us; the launch traced here: 37.1 us
  Pallas kernels  23.2 us (62%)
  starting transfers between devices  9.87 us (26%)
  other arithmetic  3.03 us (8%)
  local copies, waits for them, and re-layouts  0.88 us (2%)
    pallas_call x5, Pallas kernels, call(): pl.pallas_call(kernel, out_shape=outs, in_specs=[VM] * 6, out_specs=VM, s...  19.7 us
    ppermute x4, starting transfers between devices, send_on(): lax.ppermute(up, 'row', forward)  4.87 us
    pallas_call x1, Pallas kernels, body(): pl.pallas_call(first_kernel, out_shape=(acc_shape, shape((nc, cells, 16),...  3.53 us
    ppermute x4, starting transfers between devices, send_on(): lax.ppermute(down, 'row', backward)  2.14 us
    ppermute x1, starting transfers between devices, body(): received = lax.ppermute(send, 'col', [(0, 1), (1, 0)])  1.9 us
    concatenate x1, other arithmetic, body(): packet = jnp.concatenate([currents, geometry, spare], 1)  0.99 us
    ppermute x1, starting transfers between devices, body(): other = lax.ppermute(packet[:, COLS:PACK], 'col', [(0, 1), (1, 0)])  0.96 us
    concatenate x1, other arithmetic, body(): lists = lax.optimization_barrier(jnp.concatenate([pair_count, pair_target]))  0.76 us
  transfers between devices with their start and end apart: 10, of which 0 were waited for; matrix products, arithmetic and copies ran while one was open for 4% of the time, Pallas kernels for 58%

profile of v5, /device:TPU:1, one launch (start us, length us, event | category | flops | bytes accessed | tf_op | source)
XLA Modules:
  0.0 37.1 jit_solution(16785951235419966320)
XLA Ops:
  0.0 0.7 %copy.10 = bf16[2,7,512]{2,1,0:T(8,128)(2,1)S(1)} copy(bf16[2,7,512]{2,0,1:T(2,128)(2,1)} %param.4) | data formatting | bytes 28672 | tf_op args[0]
  0.7 0.1 pad.5.clone
  0.8 1.0 %maximum_maximum_fusion.packet = bf16[2,72,512]{2,1,0:T(8,128)(2,1)S(1)} fusion(bf16[2,7,512]{2,1,0:T(8,128)(2,1)S(1)} %copy.10, bf16[2,64,512]{2,1,0:T(8,128)(2,1)} %param.5, bf16[72]{0:T(256)(128)(2,1)S(1)} %pad.5.clone), kind=kLoop, calls=%fused_computation | loop fusion | flops 442368 | bytes 293008 | tf_op jit(solution)/shard_map/concatenate | solution.py:100
  1.8 2.1 %collective-permute-start.1 = (bf16[2,72,512]{2,1,0:T(8,128)(2,1)S(1)}, bf16[2,72,512]{2,1,0:T(8,128)(2,1)S(1)}, u32[]{:S(2)}, u32[]{:S(2)}) collective-permute-start(bf16[2,72,512]{2,1,0:T(8,128)(2,1)S(1)} %maximum_maximum_fusion.packet), channel_id=1, source_target_pairs={{4,0},{8,4},{12,8},{14,12},{10,14},{6,10},{2,6},{0,2},{5,1},{9,5},... | collective-permute-start | bytes 442376 | tf_op jit(solution)/shard_map/ppermute | solution.py:160
  3.9 0.1 collective-permute-start
  4.0 1.0 %collective-permute-start.2 = (bf16[2,8,512]{2,1,0:T(8,128)(2,1)S(1)}, bf16[2,8,512]{2,1,0:T(8,128)(2,1)S(1)}, u32[]{:S(2)}, u32[]{:S(2)}) collective-permute-start(bf16[2,8,512]{2,1,0:T(8,128)(2,1)S(1)} %concatenate.10), channel_id=1, source_target_pairs={{0,1},{1,0},{2,3},{3,2},{4,5},{5,4},{6,7},{7,6},{8,9},{9,8},{10,11... | collective-permute-start | bytes 49160 | tf_op jit(solution)/shard_map/ppermute | solution.py:101
  5.0 0.8 %pad_add_fusion = s32[208]{0:T(256)S(1)} fusion(s32[192]{0:T(256)} %param.7, s32[16]{0:T(128)} %param.6), kind=kLoop, calls=%fused_computation.22 | loop fusion | flops 208 | bytes 1664 | tf_op jit(solution)/shard_map/concatenate | solution.py:117
  5.8 0.1 select_reduce_fusion
  5.9 0.1 convert_reduce_fusion
  6.0 0.1 multiply_add_fusion.1
  6.1 0.1 broadcast_add_fusion
  6.2 0.2 add_reduce_fusion
  6.3 0.0 collective-permute-done.2.other
  6.3 0.1 broadcast_in_dim.19.weights
  6.4 3.5 %shard_map.46 = (f32[2,1024,64]{2,1,0:T(8,128)S(1)}, bf16[2,1024,16]{2,1,0:T(8,128)(2,1)S(1)}, f32[2,3,1024,128]{3,2,1,0:T(8,128)S(1)}) custom-call(bf16[2,72,512]{2,1,0:T(8,128)(2,1)S(1)} %maximum_maximum_fusion.packet, bf16[2,8,512]{2,1,0:T(8,128)(2,1)S(1)} %collective-permute-done.2.other, f32[2,16,64]{2,1,0:T(8,128)S(1)} %broadcast_in_dim.19.weights), custom_call_target="tpu_custom_call" | custom-call | flops 1258291200 | bytes 1048576 | tf_op jit(solution)/shard_map/pallas_call | solution.py:136
  9.9 0.0 collective-permute-done.1.down
  9.9 0.0 collective-permute-done.up
  9.9 1.7 %collective-permute-start.3 = (bf16[2,72,512]{2,1,0:T(8,128)(2,1)S(1)}, bf16[2,72,512]{2,1,0:T(8,128)(2,1)S(1)}, u32[]{:S(2)}, u32[]{:S(2)}) collective-permute-start(bf16[2,72,512]{2,1,0:T(8,128)(2,1)S(1)} %collective-permute-done.up), channel_id=1, source_target_pairs={{0,4},{4,8},{8,12},{12,14},{14,10},{10,6},{6,2},{2,0},{1,5},{5,9},... | collective-permute-start | bytes 442376 | tf_op jit(solution)/shard_map/ppermute | solution.py:160
  11.7 0.0 collective-permute-start.4
  11.7 5.5 %shard_map.47.acc_in = f32[2,1024,64]{2,1,0:T(8,128)S(1)} custom-call(bf16[2,72,512]{2,1,0:T(8,128)(2,1)S(1)} %collective-permute-done.up, bf16[2,72,512]{2,1,0:T(8,128)(2,1)S(1)} %collective-permute-done.1.down, f32[2,16,64]{2,1,0:T(8,128)S(1)} %broadcast_in_dim.19.weights, ...), custom_call_target="tpu_custom_call", output_to_operand_aliasing={{}: (5, {})} | custom-call | flops 2516582400 | bytes 1048576 | tf_op jit(solution)/shard_map/pallas_call | solution.py:146
  17.1 0.0 collective-permute-done.3.up
  17.1 0.0 collective-permute-done.4.down
  17.2 1.5 %collective-permute-start.5 = (bf16[2,72,512]{2,1,0:T(8,128)(2,1)S(1)}, bf16[2,72,512]{2,1,0:T(8,128)(2,1)S(1)}, u32[]{:S(2)}, u32[]{:S(2)}) collective-permute-start(bf16[2,72,512]{2,1,0:T(8,128)(2,1)S(1)} %collective-permute-done.3.up), channel_id=1, source_target_pairs={{0,4},{4,8},{8,12},{12,14},{14,10},{10,6},{6,2},{2,0},{1,5},{5,9},... | collective-permute-start | bytes 442376 | tf_op jit(solution)/shard_map/ppermute | solution.py:160
  18.7 0.0 collective-permute-start.6
  18.7 5.5 %shard_map.48.acc_in = f32[2,1024,64]{2,1,0:T(8,128)S(1)} custom-call(bf16[2,72,512]{2,1,0:T(8,128)(2,1)S(1)} %collective-permute-done.3.up, bf16[2,72,512]{2,1,0:T(8,128)(2,1)S(1)} %collective-permute-done.4.down, f32[2,16,64]{2,1,0:T(8,128)S(1)} %broadcast_in_dim.19.weights, ...), custom_call_target="tpu_custom_call", output_to_operand_aliasing={{}: (5, {})} | custom-call | flops 2516582400 | bytes 1048576 | tf_op jit(solution)/shard_map/pallas_call | solution.py:146
  24.1 0.0 collective-permute-done.5.up
  24.1 0.0 collective-permute-done.6.down
  24.2 1.5 %collective-permute-start.7 = (bf16[1,72,512]{2,1,0:T(8,128)(2,1)S(1)}, bf16[1,72,512]{2,1,0:T(8,128)(2,1)S(1)}, u32[]{:S(2)}, u32[]{:S(2)}) collective-permute-start(bf16[1,72,512]{2,1,0:T(8,128)(2,1)S(1)} %slice.16), channel_id=1, source_target_pairs={{0,4},{4,8},{8,12},{12,14},{14,10},{10,6},{6,2},{2,0},{1,5},{5,9},... | collective-permute-start | bytes 221192 | tf_op jit(solution)/shard_map/ppermute | solution.py:160
  25.7 0.0 collective-permute-start.8
  25.7 5.4 %shard_map.49.acc_in = f32[2,1024,64]{2,1,0:T(8,128)S(1)} custom-call(bf16[2,72,512]{2,1,0:T(8,128)(2,1)S(1)} %collective-permute-done.5.up, bf16[2,72,512]{2,1,0:T(8,128)(2,1)S(1)} %collective-permute-done.6.down, f32[2,16,64]{2,1,0:T(8,128)S(1)} %broadcast_in_dim.19.weights, ...), custom_call_target="tpu_custom_call", output_to_operand_aliasing={{}: (5, {})} | custom-call | flops 2516582400 | bytes 1048576 | tf_op jit(solution)/shard_map/pallas_call | solution.py:146
  31.2 0.0 collective-permute-done.7.up
  31.2 0.0 collective-permute-done.8.down
  31.2 1.7 %shard_map.51 = f32[2,64,512]{2,1,0:T(8,128)S(1)} custom-call(bf16[1,72,512]{2,1,0:T(8,128)(2,1)S(1)} %collective-permute-done.7.up, bf16[1,72,512]{2,1,0:T(8,128)(2,1)S(1)} %collective-permute-done.8.down, f32[2,16,64]{2,1,0:T(8,128)S(1)} %broadcast_in_dim.19.weights, bf16[2,1024,16]{2,1,0:T(8,128)(2,1)S(1)} %get-tuple-element.20.left, ...), custom_call_target="tpu_custom_call" | custom-call | flops 1258291200 | bytes 1048576 | tf_op jit(solution)/shard_map/pallas_call | solution.py:146
  32.8 1.9 %collective-permute-start.9 = (f32[2,64,512]{2,1,0:T(8,128)S(1)}, f32[2,64,512]{2,1,0:T(8,128)S(1)}, u32[]{:S(2)}, u32[]{:S(2)}) collective-permute-start(f32[2,64,512]{2,1,0:T(8,128)S(1)} %shard_map.51), channel_id=1, source_target_pairs={{0,1},{1,0},{2,3},{3,2},{4,5},{5,4},{6,7},{7,6},{8,9},{9,8},{10,11... | collective-permute-start | bytes 786440 | tf_op jit(solution)/shard_map/ppermute | solution.py:174
  34.7 1.6 %shard_map.50 = f32[2,64,512]{2,1,0:T(8,128)S(1)} custom-call(bf16[1,72,512]{2,1,0:T(8,128)(2,1)S(1)} %collective-permute-done.7.up, bf16[1,72,512]{2,1,0:T(8,128)(2,1)S(1)} %collective-permute-done.8.down, f32[2,16,64]{2,1,0:T(8,128)S(1)} %broadcast_in_dim.19.weights, bf16[2,1024,16]{2,1,0:T(8,128)(2,1)S(1)} %get-tuple-element.20.left, ...), custom_call_target="tpu_custom_call" | custom-call | flops 1258291200 | bytes 1048576 | tf_op jit(solution)/shard_map/pallas_call | solution.py:146
  36.4 0.0 collective-permute-done.9
  36.4 0.7 %add.143 = f32[2,64,512]{2,1,0:T(8,128)} add(f32[2,64,512]{2,1,0:T(8,128)S(1)} %shard_map.50, f32[2,64,512]{2,1,0:T(8,128)S(1)} %collective-permute-done.9) | non-fusion elementwise | flops 65536 | bytes 786432 | tf_op jit(solution)/shard_map/add | solution.py:176
  (6 shorter events, 0.1 us)
Async XLA Ops:
  1.8 8.1 %collective-permute-start.1 = (bf16[2,72,512]{2,1,0:T(8,128)(2,1)S(1)}, bf16[2,72,512]{2,1,0:T(8,128)(2,1)S(1)}, u32[]{:S(2)}, u32[]{:S(2)}) collective-permute-start(bf16[2,72,512]{2,1,0:T(8,128)(2,1)S(1)} %maximum_maximum_fusion.packet), channel_id=1, source_target_pairs={{4,0},{8,4},{12,8},{14,12},{10,14},{6,10},{2,6},{0,2},{5,1},{9,5},... | collective-permute-start | bytes 442376 | tf_op jit(solution)/shard_map/ppermute | solution.py:160
  3.9 6.0 %collective-permute-start = (bf16[2,72,512]{2,1,0:T(8,128)(2,1)S(1)}, bf16[2,72,512]{2,1,0:T(8,128)(2,1)S(1)}, u32[]{:S(2)}, u32[]{:S(2)}) collective-permute-start(bf16[2,72,512]{2,1,0:T(8,128)(2,1)S(1)} %maximum_maximum_fusion.packet), channel_id=1, source_target_pairs={{0,4},{4,8},{8,12},{12,14},{14,10},{10,6},{6,2},{2,0},{1,5},{5,9},... | collective-permute-start | bytes 442376 | tf_op jit(solution)/shard_map/ppermute | solution.py:160
  4.0 2.3 %collective-permute-start.2 = (bf16[2,8,512]{2,1,0:T(8,128)(2,1)S(1)}, bf16[2,8,512]{2,1,0:T(8,128)(2,1)S(1)}, u32[]{:S(2)}, u32[]{:S(2)}) collective-permute-start(bf16[2,8,512]{2,1,0:T(8,128)(2,1)S(1)} %concatenate.10), channel_id=1, source_target_pairs={{0,1},{1,0},{2,3},{3,2},{4,5},{5,4},{6,7},{7,6},{8,9},{9,8},{10,11... | collective-permute-start | bytes 49160 | tf_op jit(solution)/shard_map/ppermute | solution.py:101
  9.9 7.2 %collective-permute-start.3 = (bf16[2,72,512]{2,1,0:T(8,128)(2,1)S(1)}, bf16[2,72,512]{2,1,0:T(8,128)(2,1)S(1)}, u32[]{:S(2)}, u32[]{:S(2)}) collective-permute-start(bf16[2,72,512]{2,1,0:T(8,128)(2,1)S(1)} %collective-permute-done.up), channel_id=1, source_target_pairs={{0,4},{4,8},{8,12},{12,14},{14,10},{10,6},{6,2},{2,0},{1,5},{5,9},... | collective-permute-start | bytes 442376 | tf_op jit(solution)/shard_map/ppermute | solution.py:160
  11.7 5.5 %collective-permute-start.4 = (bf16[2,72,512]{2,1,0:T(8,128)(2,1)S(1)}, bf16[2,72,512]{2,1,0:T(8,128)(2,1)S(1)}, u32[]{:S(2)}, u32[]{:S(2)}) collective-permute-start(bf16[2,72,512]{2,1,0:T(8,128)(2,1)S(1)} %collective-permute-done.1.down), channel_id=1, source_target_pairs={{4,0},{8,4},{12,8},{14,12},{10,14},{6,10},{2,6},{0,2},{5,1},{9,5},... | collective-permute-start | bytes 442376 | tf_op jit(solution)/shard_map/ppermute | solution.py:160
  17.2 7.0 %collective-permute-start.5 = (bf16[2,72,512]{2,1,0:T(8,128)(2,1)S(1)}, bf16[2,72,512]{2,1,0:T(8,128)(2,1)S(1)}, u32[]{:S(2)}, u32[]{:S(2)}) collective-permute-start(bf16[2,72,512]{2,1,0:T(8,128)(2,1)S(1)} %collective-permute-done.3.up), channel_id=1, source_target_pairs={{0,4},{4,8},{8,12},{12,14},{14,10},{10,6},{6,2},{2,0},{1,5},{5,9},... | collective-permute-start | bytes 442376 | tf_op jit(solution)/shard_map/ppermute | solution.py:160
  18.7 5.5 %collective-permute-start.6 = (bf16[2,72,512]{2,1,0:T(8,128)(2,1)S(1)}, bf16[2,72,512]{2,1,0:T(8,128)(2,1)S(1)}, u32[]{:S(2)}, u32[]{:S(2)}) collective-permute-start(bf16[2,72,512]{2,1,0:T(8,128)(2,1)S(1)} %collective-permute-done.4.down), channel_id=1, source_target_pairs={{4,0},{8,4},{12,8},{14,12},{10,14},{6,10},{2,6},{0,2},{5,1},{9,5},... | collective-permute-start | bytes 442376 | tf_op jit(solution)/shard_map/ppermute | solution.py:160
  24.2 7.0 %collective-permute-start.7 = (bf16[1,72,512]{2,1,0:T(8,128)(2,1)S(1)}, bf16[1,72,512]{2,1,0:T(8,128)(2,1)S(1)}, u32[]{:S(2)}, u32[]{:S(2)}) collective-permute-start(bf16[1,72,512]{2,1,0:T(8,128)(2,1)S(1)} %slice.16), channel_id=1, source_target_pairs={{0,4},{4,8},{8,12},{12,14},{14,10},{10,6},{6,2},{2,0},{1,5},{5,9},... | collective-permute-start | bytes 221192 | tf_op jit(solution)/shard_map/ppermute | solution.py:160
  25.7 5.5 %collective-permute-start.8 = (bf16[1,72,512]{2,1,0:T(8,128)(2,1)S(1)}, bf16[1,72,512]{2,1,0:T(8,128)(2,1)S(1)}, u32[]{:S(2)}, u32[]{:S(2)}) collective-permute-start(bf16[1,72,512]{2,1,0:T(8,128)(2,1)S(1)} %slice.17), channel_id=1, source_target_pairs={{4,0},{8,4},{12,8},{14,12},{10,14},{6,10},{2,6},{0,2},{5,1},{9,5},... | collective-permute-start | bytes 221192 | tf_op jit(solution)/shard_map/ppermute | solution.py:160
  32.8 3.6 %collective-permute-start.9 = (f32[2,64,512]{2,1,0:T(8,128)S(1)}, f32[2,64,512]{2,1,0:T(8,128)S(1)}, u32[]{:S(2)}, u32[]{:S(2)}) collective-permute-start(f32[2,64,512]{2,1,0:T(8,128)S(1)} %shard_map.51), channel_id=1, source_target_pairs={{0,1},{1,0},{2,3},{3,2},{4,5},{5,4},{6,7},{7,6},{8,9},{9,8},{10,11... | collective-permute-start | bytes 786440 | tf_op jit(solution)/shard_map/ppermute | solution.py:174

commit v6 on v5

--- a/solution.py
+++ b/solution.py
@@ -102,12 +102,14 @@
 
     ring = ring_of(n)
     forward = [(ring[i], ring[(i + 1) % n]) for i in range(n)]
-    backward = [(b, a) for a, b in forward]
+    there = [(2 * a, 2 * b) for a, b in forward] + [(2 * b + 1, 2 * a + 1) for a, b in forward]
+    back = [(b, a) for a, b in there]
     steps = n // 2
     row = lax.axis_index("row")
     own = row * nc + jnp.arange(nc)
     turn = jnp.arange(n * nc) // nc
     shift = jnp.where(turn % 2 == 1, -((turn + 1) // 2), turn // 2)
+    shift = jnp.where(lax.axis_index("col") == 1, -shift, shift)
     if n == 8:
         spot = (jnp.where(row % 2 == 0, row // 2, n - 1 - row // 2) + shift + n) % n
         chip = jnp.where(spot < n // 2, 2 * spot, 2 * (n - 1 - spot) + 1)
@@ -157,7 +159,7 @@
     def send_on(s, up, down):
         if s == steps:
             up, down = up[: nc // 2], down[nc // 2 :]
-        return lax.ppermute(up, "row", forward), lax.ppermute(down, "row", backward)
+        return lax.ppermute(up, ("row", "col"), there), lax.ppermute(down, ("row", "col"), back)
 
     up, down = send_on(1, packet, packet)
     offset = nc

time: 37.4 us -> 37 us (0.989)
    ppermute x1, starting transfers between devices: 1.9 us -> 1.48 us  [body(): received = lax.ppermute(send, 'col', [(0, 1), (1, 0)])]
where the time goes in v6:
time: 37 us; the launch traced here: 36.8 us
  Pallas kernels  23.2 us (63%)
  starting transfers between devices  9.52 us (26%)
  other arithmetic  3.04 us (8%)
  local copies, waits for them, and re-layouts  0.88 us (2%)
    pallas_call x5, Pallas kernels, call(): pl.pallas_call(kernel, out_shape=outs, in_specs=[VM] * 6, out_specs=VM, s...  19.6 us
    ppermute x4, starting transfers between devices, send_on(): lax.ppermute(up, ('row', 'col'), there)  4.44 us
    pallas_call x1, Pallas kernels, body(): pl.pallas_call(first_kernel, out_shape=(acc_shape, shape((nc, cells, 16),...  3.53 us
    ppermute x4, starting transfers between devices, send_on(): lax.ppermute(down, ('row', 'col'), back)  2.59 us
    ppermute x1, starting transfers between devices, body(): received = lax.ppermute(send, 'col', [(0, 1), (1, 0)])  1.48 us
    ppermute x1, starting transfers between devices, body(): other = lax.ppermute(packet[:, COLS:PACK], 'col', [(0, 1), (1, 0)])  1.01 us
    concatenate x1, other arithmetic, body(): packet = jnp.concatenate([currents, geometry, spare], 1)  0.99 us
    concatenate x1, other arithmetic, body(): lists = lax.optimization_barrier(jnp.concatenate([pair_count, pair_target]))  0.75 us
  transfers between devices with their start and end apart: 10, of which 0 were waited for; matrix products, arithmetic and copies ran while one was open for 4% of the time, Pallas kernels for 58%

profile of v6, /device:TPU:1, one launch (start us, length us, event | category | flops | bytes accessed | tf_op | source)
XLA Modules:
  0.0 36.8 jit_solution(17515328876461785752)
XLA Ops:
  0.0 0.7 %copy.10 = bf16[2,7,512]{2,1,0:T(8,128)(2,1)S(1)} copy(bf16[2,7,512]{2,0,1:T(2,128)(2,1)} %param.4) | data formatting | bytes 28672 | tf_op args[0]
  0.7 0.1 pad.5.clone
  0.8 1.0 %maximum_maximum_fusion.packet = bf16[2,72,512]{2,1,0:T(8,128)(2,1)S(1)} fusion(bf16[2,7,512]{2,1,0:T(8,128)(2,1)S(1)} %copy.10, bf16[2,64,512]{2,1,0:T(8,128)(2,1)} %param.5, bf16[72]{0:T(256)(128)(2,1)S(1)} %pad.5.clone), kind=kLoop, calls=%fused_computation | loop fusion | flops 442368 | bytes 293008 | tf_op jit(solution)/shard_map/concatenate | solution.py:100
  1.8 2.2 %collective-permute-start.1 = (bf16[2,72,512]{2,1,0:T(8,128)(2,1)S(1)}, bf16[2,72,512]{2,1,0:T(8,128)(2,1)S(1)}, u32[]{:S(2)}, u32[]{:S(2)}) collective-permute-start(bf16[2,72,512]{2,1,0:T(8,128)(2,1)S(1)} %maximum_maximum_fusion.packet), channel_id=1, source_target_pairs={{4,0},{8,4},{12,8},{14,12},{10,14},{6,10},{2,6},{0,2},{1,5},{5,9},... | collective-permute-start | bytes 442376 | tf_op jit(solution)/shard_map/ppermute | solution.py:162
  4.0 0.0 collective-permute-start
  4.0 1.0 %collective-permute-start.2 = (bf16[2,8,512]{2,1,0:T(8,128)(2,1)S(1)}, bf16[2,8,512]{2,1,0:T(8,128)(2,1)S(1)}, u32[]{:S(2)}, u32[]{:S(2)}) collective-permute-start(bf16[2,8,512]{2,1,0:T(8,128)(2,1)S(1)} %concatenate.10), channel_id=1, source_target_pairs={{0,1},{1,0},{2,3},{3,2},{4,5},{5,4},{6,7},{7,6},{8,9},{9,8},{10,11... | collective-permute-start | bytes 49160 | tf_op jit(solution)/shard_map/ppermute | solution.py:101
  5.0 0.8 %pad_add_fusion = s32[208]{0:T(256)S(1)} fusion(s32[192]{0:T(256)} %param.7, s32[16]{0:T(128)} %param.6), kind=kLoop, calls=%fused_computation.22 | loop fusion | flops 208 | bytes 1664 | tf_op jit(solution)/shard_map/concatenate | solution.py:119
  5.8 0.1 select_reduce_fusion
  5.9 0.1 convert_reduce_fusion
  6.0 0.1 multiply_add_fusion.1
  6.1 0.1 broadcast_add_fusion
  6.1 0.2 add_reduce_fusion
  6.3 0.0 collective-permute-done.2.other
  6.3 0.1 broadcast_in_dim.19.weights
  6.4 3.5 %shard_map.46 = (f32[2,1024,64]{2,1,0:T(8,128)S(1)}, bf16[2,1024,16]{2,1,0:T(8,128)(2,1)S(1)}, f32[2,3,1024,128]{3,2,1,0:T(8,128)S(1)}) custom-call(bf16[2,72,512]{2,1,0:T(8,128)(2,1)S(1)} %maximum_maximum_fusion.packet, bf16[2,8,512]{2,1,0:T(8,128)(2,1)S(1)} %collective-permute-done.2.other, f32[2,16,64]{2,1,0:T(8,128)S(1)} %broadcast_in_dim.19.weights), custom_call_target="tpu_custom_call" | custom-call | flops 1258291200 | bytes 1048576 | tf_op jit(solution)/shard_map/pallas_call | solution.py:138
  9.9 0.0 collective-permute-done.1.down
  9.9 0.0 collective-permute-done.up
  9.9 1.7 %collective-permute-start.3 = (bf16[2,72,512]{2,1,0:T(8,128)(2,1)S(1)}, bf16[2,72,512]{2,1,0:T(8,128)(2,1)S(1)}, u32[]{:S(2)}, u32[]{:S(2)}) collective-permute-start(bf16[2,72,512]{2,1,0:T(8,128)(2,1)S(1)} %collective-permute-done.up), channel_id=1, source_target_pairs={{0,4},{4,8},{8,12},{12,14},{14,10},{10,6},{6,2},{2,0},{5,1},{9,5},... | collective-permute-start | bytes 442376 | tf_op jit(solution)/shard_map/ppermute | solution.py:162
  11.6 0.1 collective-permute-start.4
  11.7 5.5 %shard_map.47.acc_in = f32[2,1024,64]{2,1,0:T(8,128)S(1)} custom-call(bf16[2,72,512]{2,1,0:T(8,128)(2,1)S(1)} %collective-permute-done.up, bf16[2,72,512]{2,1,0:T(8,128)(2,1)S(1)} %collective-permute-done.1.down, f32[2,16,64]{2,1,0:T(8,128)S(1)} %broadcast_in_dim.19.weights, ...), custom_call_target="tpu_custom_call", output_to_operand_aliasing={{}: (5, {})} | custom-call | flops 2516582400 | bytes 1048576 | tf_op jit(solution)/shard_map/pallas_call | solution.py:148
  17.2 0.0 collective-permute-done.3.up
  17.2 0.0 collective-permute-done.4.down
  17.2 1.4 %collective-permute-start.5 = (bf16[2,72,512]{2,1,0:T(8,128)(2,1)S(1)}, bf16[2,72,512]{2,1,0:T(8,128)(2,1)S(1)}, u32[]{:S(2)}, u32[]{:S(2)}) collective-permute-start(bf16[2,72,512]{2,1,0:T(8,128)(2,1)S(1)} %collective-permute-done.3.up), channel_id=1, source_target_pairs={{0,4},{4,8},{8,12},{12,14},{14,10},{10,6},{6,2},{2,0},{5,1},{9,5},... | collective-permute-start | bytes 442376 | tf_op jit(solution)/shard_map/ppermute | solution.py:162
  18.6 0.1 collective-permute-start.6
  18.7 5.5 %shard_map.48.acc_in = f32[2,1024,64]{2,1,0:T(8,128)S(1)} custom-call(bf16[2,72,512]{2,1,0:T(8,128)(2,1)S(1)} %collective-permute-done.3.up, bf16[2,72,512]{2,1,0:T(8,128)(2,1)S(1)} %collective-permute-done.4.down, f32[2,16,64]{2,1,0:T(8,128)S(1)} %broadcast_in_dim.19.weights, ...), custom_call_target="tpu_custom_call", output_to_operand_aliasing={{}: (5, {})} | custom-call | flops 2516582400 | bytes 1048576 | tf_op jit(solution)/shard_map/pallas_call | solution.py:148
  24.2 0.0 collective-permute-done.5.up
  24.2 0.0 collective-permute-done.6.down
  24.2 1.4 %collective-permute-start.7 = (bf16[1,72,512]{2,1,0:T(8,128)(2,1)S(1)}, bf16[1,72,512]{2,1,0:T(8,128)(2,1)S(1)}, u32[]{:S(2)}, u32[]{:S(2)}) collective-permute-start(bf16[1,72,512]{2,1,0:T(8,128)(2,1)S(1)} %slice.16), channel_id=1, source_target_pairs={{0,4},{4,8},{8,12},{12,14},{14,10},{10,6},{6,2},{2,0},{5,1},{9,5},... | collective-permute-start | bytes 221192 | tf_op jit(solution)/shard_map/ppermute | solution.py:162
  25.6 0.1 collective-permute-start.8
  25.8 5.4 %shard_map.49.acc_in = f32[2,1024,64]{2,1,0:T(8,128)S(1)} custom-call(bf16[2,72,512]{2,1,0:T(8,128)(2,1)S(1)} %collective-permute-done.5.up, bf16[2,72,512]{2,1,0:T(8,128)(2,1)S(1)} %collective-permute-done.6.down, f32[2,16,64]{2,1,0:T(8,128)S(1)} %broadcast_in_dim.19.weights, ...), custom_call_target="tpu_custom_call", output_to_operand_aliasing={{}: (5, {})} | custom-call | flops 2516582400 | bytes 1048576 | tf_op jit(solution)/shard_map/pallas_call | solution.py:148
  31.2 0.0 collective-permute-done.7.up
  31.2 0.0 collective-permute-done.8.down
  31.2 1.7 %shard_map.51 = f32[2,64,512]{2,1,0:T(8,128)S(1)} custom-call(bf16[1,72,512]{2,1,0:T(8,128)(2,1)S(1)} %collective-permute-done.7.up, bf16[1,72,512]{2,1,0:T(8,128)(2,1)S(1)} %collective-permute-done.8.down, f32[2,16,64]{2,1,0:T(8,128)S(1)} %broadcast_in_dim.19.weights, bf16[2,1024,16]{2,1,0:T(8,128)(2,1)S(1)} %get-tuple-element.20.left, ...), custom_call_target="tpu_custom_call" | custom-call | flops 1258291200 | bytes 1048576 | tf_op jit(solution)/shard_map/pallas_call | solution.py:148
  32.9 1.5 %collective-permute-start.9 = (f32[2,64,512]{2,1,0:T(8,128)S(1)}, f32[2,64,512]{2,1,0:T(8,128)S(1)}, u32[]{:S(2)}, u32[]{:S(2)}) collective-permute-start(f32[2,64,512]{2,1,0:T(8,128)S(1)} %shard_map.51), channel_id=1, source_target_pairs={{0,1},{1,0},{2,3},{3,2},{4,5},{5,4},{6,7},{7,6},{8,9},{9,8},{10,11... | collective-permute-start | bytes 786440 | tf_op jit(solution)/shard_map/ppermute | solution.py:176
  34.4 1.6 %shard_map.50 = f32[2,64,512]{2,1,0:T(8,128)S(1)} custom-call(bf16[1,72,512]{2,1,0:T(8,128)(2,1)S(1)} %collective-permute-done.7.up, bf16[1,72,512]{2,1,0:T(8,128)(2,1)S(1)} %collective-permute-done.8.down, f32[2,16,64]{2,1,0:T(8,128)S(1)} %broadcast_in_dim.19.weights, bf16[2,1024,16]{2,1,0:T(8,128)(2,1)S(1)} %get-tuple-element.20.left, ...), custom_call_target="tpu_custom_call" | custom-call | flops 1258291200 | bytes 1048576 | tf_op jit(solution)/shard_map/pallas_call | solution.py:148
  36.0 0.0 collective-permute-done.9
  36.0 0.7 %add.147 = f32[2,64,512]{2,1,0:T(8,128)} add(f32[2,64,512]{2,1,0:T(8,128)S(1)} %shard_map.50, f32[2,64,512]{2,1,0:T(8,128)S(1)} %collective-permute-done.9) | non-fusion elementwise | flops 65536 | bytes 786432 | tf_op jit(solution)/shard_map/add | solution.py:178
  (6 shorter events, 0.1 us)
Async XLA Ops:
  1.8 8.1 %collective-permute-start.1 = (bf16[2,72,512]{2,1,0:T(8,128)(2,1)S(1)}, bf16[2,72,512]{2,1,0:T(8,128)(2,1)S(1)}, u32[]{:S(2)}, u32[]{:S(2)}) collective-permute-start(bf16[2,72,512]{2,1,0:T(8,128)(2,1)S(1)} %maximum_maximum_fusion.packet), channel_id=1, source_target_pairs={{4,0},{8,4},{12,8},{14,12},{10,14},{6,10},{2,6},{0,2},{1,5},{5,9},... | collective-permute-start | bytes 442376 | tf_op jit(solution)/shard_map/ppermute | solution.py:162
  4.0 6.0 %collective-permute-start = (bf16[2,72,512]{2,1,0:T(8,128)(2,1)S(1)}, bf16[2,72,512]{2,1,0:T(8,128)(2,1)S(1)}, u32[]{:S(2)}, u32[]{:S(2)}) collective-permute-start(bf16[2,72,512]{2,1,0:T(8,128)(2,1)S(1)} %maximum_maximum_fusion.packet), channel_id=1, source_target_pairs={{0,4},{4,8},{8,12},{12,14},{14,10},{10,6},{6,2},{2,0},{5,1},{9,5},... | collective-permute-start | bytes 442376 | tf_op jit(solution)/shard_map/ppermute | solution.py:162
  4.0 2.3 %collective-permute-start.2 = (bf16[2,8,512]{2,1,0:T(8,128)(2,1)S(1)}, bf16[2,8,512]{2,1,0:T(8,128)(2,1)S(1)}, u32[]{:S(2)}, u32[]{:S(2)}) collective-permute-start(bf16[2,8,512]{2,1,0:T(8,128)(2,1)S(1)} %concatenate.10), channel_id=1, source_target_pairs={{0,1},{1,0},{2,3},{3,2},{4,5},{5,4},{6,7},{7,6},{8,9},{9,8},{10,11... | collective-permute-start | bytes 49160 | tf_op jit(solution)/shard_map/ppermute | solution.py:101
  9.9 7.3 %collective-permute-start.3 = (bf16[2,72,512]{2,1,0:T(8,128)(2,1)S(1)}, bf16[2,72,512]{2,1,0:T(8,128)(2,1)S(1)}, u32[]{:S(2)}, u32[]{:S(2)}) collective-permute-start(bf16[2,72,512]{2,1,0:T(8,128)(2,1)S(1)} %collective-permute-done.up), channel_id=1, source_target_pairs={{0,4},{4,8},{8,12},{12,14},{14,10},{10,6},{6,2},{2,0},{5,1},{9,5},... | collective-permute-start | bytes 442376 | tf_op jit(solution)/shard_map/ppermute | solution.py:162
  11.6 5.6 %collective-permute-start.4 = (bf16[2,72,512]{2,1,0:T(8,128)(2,1)S(1)}, bf16[2,72,512]{2,1,0:T(8,128)(2,1)S(1)}, u32[]{:S(2)}, u32[]{:S(2)}) collective-permute-start(bf16[2,72,512]{2,1,0:T(8,128)(2,1)S(1)} %collective-permute-done.1.down), channel_id=1, source_target_pairs={{4,0},{8,4},{12,8},{14,12},{10,14},{6,10},{2,6},{0,2},{1,5},{5,9},... | collective-permute-start | bytes 442376 | tf_op jit(solution)/shard_map/ppermute | solution.py:162
  17.2 7.0 %collective-permute-start.5 = (bf16[2,72,512]{2,1,0:T(8,128)(2,1)S(1)}, bf16[2,72,512]{2,1,0:T(8,128)(2,1)S(1)}, u32[]{:S(2)}, u32[]{:S(2)}) collective-permute-start(bf16[2,72,512]{2,1,0:T(8,128)(2,1)S(1)} %collective-permute-done.3.up), channel_id=1, source_target_pairs={{0,4},{4,8},{8,12},{12,14},{14,10},{10,6},{6,2},{2,0},{5,1},{9,5},... | collective-permute-start | bytes 442376 | tf_op jit(solution)/shard_map/ppermute | solution.py:162
  18.6 5.6 %collective-permute-start.6 = (bf16[2,72,512]{2,1,0:T(8,128)(2,1)S(1)}, bf16[2,72,512]{2,1,0:T(8,128)(2,1)S(1)}, u32[]{:S(2)}, u32[]{:S(2)}) collective-permute-start(bf16[2,72,512]{2,1,0:T(8,128)(2,1)S(1)} %collective-permute-done.4.down), channel_id=1, source_target_pairs={{4,0},{8,4},{12,8},{14,12},{10,14},{6,10},{2,6},{0,2},{1,5},{5,9},... | collective-permute-start | bytes 442376 | tf_op jit(solution)/shard_map/ppermute | solution.py:162
  24.2 7.0 %collective-permute-start.7 = (bf16[1,72,512]{2,1,0:T(8,128)(2,1)S(1)}, bf16[1,72,512]{2,1,0:T(8,128)(2,1)S(1)}, u32[]{:S(2)}, u32[]{:S(2)}) collective-permute-start(bf16[1,72,512]{2,1,0:T(8,128)(2,1)S(1)} %slice.16), channel_id=1, source_target_pairs={{0,4},{4,8},{8,12},{12,14},{14,10},{10,6},{6,2},{2,0},{5,1},{9,5},... | collective-permute-start | bytes 221192 | tf_op jit(solution)/shard_map/ppermute | solution.py:162
  25.6 5.6 %collective-permute-start.8 = (bf16[1,72,512]{2,1,0:T(8,128)(2,1)S(1)}, bf16[1,72,512]{2,1,0:T(8,128)(2,1)S(1)}, u32[]{:S(2)}, u32[]{:S(2)}) collective-permute-start(bf16[1,72,512]{2,1,0:T(8,128)(2,1)S(1)} %slice.17), channel_id=1, source_target_pairs={{4,0},{8,4},{12,8},{14,12},{10,14},{6,10},{2,6},{0,2},{1,5},{5,9},... | collective-permute-start | bytes 221192 | tf_op jit(solution)/shard_map/ppermute | solution.py:162
  32.9 3.1 %collective-permute-start.9 = (f32[2,64,512]{2,1,0:T(8,128)S(1)}, f32[2,64,512]{2,1,0:T(8,128)S(1)}, u32[]{:S(2)}, u32[]{:S(2)}) collective-permute-start(f32[2,64,512]{2,1,0:T(8,128)S(1)} %shard_map.51), channel_id=1, source_target_pairs={{0,1},{1,0},{2,3},{3,2},{4,5},{5,4},{6,7},{7,6},{8,9},{9,8},{10,11... | collective-permute-start | bytes 786440 | tf_op jit(solution)/shard_map/ppermute | solution.py:176
